TPU v7x, 128 devices: a whole 4x4x4 slice. The times are simulated.
128 devices in a mesh: dp: 16 (over z, x_lo, core), graph: 8 (over y, x_hi).
Axes of the slice: x: 4 (x_hi: 2, x_lo: 2; x = x_hi * 2 + x_lo), y: 4, z: 4, core: 2. Of those that a mesh axis runs over, the one named last changes fastest.
Arguments:
- edge_feats: bfloat16 [131072, 512], P(('dp', 'graph')), may hold values from -24 to 24
- cotangent: bfloat16 [131072, 512], P(('dp', 'graph')), may hold values from -6 to 6
- angle_basis: bfloat16 [16, 1048576], P(None, ('dp', 'graph')), may hold values from -6 to 6
- source_edge: int32 [1048576], P(('dp', 'graph')), may hold values from 0 to 8191
- target_edge: int32 [1048576], P(('dp', 'graph')), may hold values from 0 to 1023
- pair_weight: bfloat16 [512, 512], P('dp'), may hold values from -0.25 to 0.25
- down_weight: bfloat16 [512, 64], P('dp'), may hold values from -0.25 to 0.25
- basis_weight: bfloat16 [16, 64], P('dp'), may hold values from -1.5 to 1.5
- up_weight: bfloat16 [64, 512], P('dp'), may hold values from -0.75 to 0.75
- res_first: bfloat16 [512, 512], P('dp'), may hold values from -0.25 to 0.25
- res_second: bfloat16 [512, 512], P('dp'), may hold values from -0.25 to 0.25
Outputs:
- edge_grad: bfloat16 [131072, 512], P(('dp', 'graph'))
- pair_grad: float32 [512, 512], P('dp')
- down_grad: float32 [512, 64], P('dp')
- basis_grad: float32 [16, 64], P('dp')
- up_grad: float32 [64, 512], P('dp')
- first_grad: float32 [512, 512], P('dp')
- second_grad: float32 [512, 512], P('dp')
Inputs may be any that keep to these rules, and one draw needn't show every extreme that they name: source_edge[t] may name any edge of the 8 devices of the triplet's group. target_edge[t] names an edge of the triplet's own device.
All inputs are finite; a program needn't handle non-finite values.
Results may differ from a plain program's by a relative error of at most 0.013.
Values may be sent and summed in bfloat16 or wider, within the bound.
No kernel may reach another device: no remote copies, remote signals or barrier semaphores. Data moves between devices by JAX's collectives and lax.ppermute only.
A program may use at most 64 MiB of HBM per device.

v0:
```python
import math

import jax
import jax.numpy as jnp
from jax import lax
from jax.sharding import PartitionSpec as P


def silu_slope(value):
    sig = jax.nn.sigmoid(value)
    return sig * (1.0 + value * (1.0 - sig))


def on_device(
    edge_feats,
    cotangent,
    angle_basis,
    source_edge,
    target_edge,
    pair_weight,
    down_weight,
    basis_weight,
    up_weight,
    res_first,
    res_second,
):
    f32 = jnp.float32
    bf16 = jnp.bfloat16
    scale = math.sqrt(0.5)
    w_pair, w_down, w_basis, w_up, w_first, w_second = (
        lax.all_gather(pair_weight, "dp", axis=0, tiled=True),
        lax.all_gather(down_weight, "dp", axis=0, tiled=True),
        lax.all_gather(basis_weight, "dp", axis=0, tiled=True),
        lax.all_gather(up_weight, "dp", axis=0, tiled=True),
        lax.all_gather(res_first, "dp", axis=0, tiled=True),
        lax.all_gather(res_second, "dp", axis=0, tiled=True),
    )
    edge_rows = edge_feats.shape[0]
    width_trip = w_down.shape[1]
    z_one = jnp.dot(edge_feats, w_pair, preferred_element_type=f32)
    hidden = jax.nn.silu(z_one).astype(bf16)
    down_t = jnp.einsum("ed,dk->ke", hidden, w_down, preferred_element_type=f32).astype(bf16)
    group_down = lax.all_gather(down_t, "graph", axis=1, tiled=True)
    group_cols = group_down.shape[1]
    coeff = jnp.einsum("nk,nt->kt", w_basis, angle_basis, preferred_element_type=f32)
    down_in = jnp.take(group_down, source_edge, axis=1).astype(f32)
    agg_t = (
        jnp.zeros((width_trip, edge_rows), f32).at[:, target_edge].add(down_in * coeff).astype(bf16)
    )
    z_two = jnp.einsum("ke,kd->ed", agg_t, w_up, preferred_element_type=f32)
    mixed = jax.nn.silu(z_two).astype(bf16)
    z_three = jnp.dot(mixed, w_first, preferred_element_type=f32)
    inner = jax.nn.silu(z_three).astype(bf16)
    z_four = jnp.dot(inner, w_second, preferred_element_type=f32)
    dz_four = (scale * cotangent.astype(f32) * silu_slope(z_four)).astype(bf16)
    dz_three = (
        jnp.einsum("ed,fd->ef", dz_four, w_second, preferred_element_type=f32) * silu_slope(z_three)
    ).astype(bf16)
    dmixed = scale * cotangent.astype(f32) + jnp.einsum(
        "ed,fd->ef", dz_three, w_first, preferred_element_type=f32
    )
    dz_two = (dmixed * silu_slope(z_two)).astype(bf16)
    dagg_t = jnp.einsum("kd,ed->ke", w_up, dz_two, preferred_element_type=f32)
    dagg_out = jnp.take(dagg_t, target_edge, axis=1)
    dcoeff = (dagg_out * down_in).astype(bf16)
    partial_down = jnp.zeros((width_trip, group_cols), f32).at[:, source_edge].add(dagg_out * coeff)
    ddown_t = lax.psum_scatter(partial_down, "graph", scatter_dimension=1, tiled=True).astype(bf16)
    second_local = jnp.einsum("ed,ef->df", inner, dz_four, preferred_element_type=f32)
    first_local = jnp.einsum("ed,ef->df", mixed, dz_three, preferred_element_type=f32)
    up_local = jnp.einsum("ke,ed->kd", agg_t, dz_two, preferred_element_type=f32)
    basis_local = jnp.einsum("nt,kt->nk", angle_basis, dcoeff, preferred_element_type=f32)
    down_local = jnp.einsum("ed,ke->dk", hidden, ddown_t, preferred_element_type=f32)
    dz_one = (
        jnp.einsum("ke,dk->ed", ddown_t, w_down, preferred_element_type=f32) * silu_slope(z_one)
    ).astype(bf16)
    pair_local = jnp.einsum("ed,ef->df", edge_feats, dz_one, preferred_element_type=f32)
    edge_grad = jnp.einsum("ef,df->ed", dz_one, w_pair, preferred_element_type=f32).astype(bf16)
    locals_all = (pair_local, down_local, basis_local, up_local, first_local, second_local)
    data_count = lax.axis_size("dp")
    packed = jnp.concatenate([item.reshape(data_count, -1) for item in locals_all], axis=1).reshape(
        -1
    )
    rows_sum = lax.psum_scatter(packed, "dp", scatter_dimension=0, tiled=True)
    shares = lax.psum(rows_sum, "graph")
    outputs = []
    offset = 0
    for item in locals_all:
        share_rows = item.shape[0] // data_count
        length = share_rows * item.shape[1]
        outputs.append(shares[offset : offset + length].reshape(share_rows, item.shape[1]))
        offset = offset + length
    return (edge_grad, outputs[0], outputs[1], outputs[2], outputs[3], outputs[4], outputs[5])


def solution(mesh):
    return jax.shard_map(
        on_device,
        mesh=mesh,
        in_specs=(
            P(("dp", "graph"), None),
            P(("dp", "graph"), None),
            P(None, ("dp", "graph")),
            P(("dp", "graph")),
            P(("dp", "graph")),
            P("dp", None),
            P("dp", None),
            P("dp", None),
            P("dp", None),
            P("dp", None),
            P("dp", None),
        ),
        out_specs=(
            P(("dp", "graph"), None),
            P("dp", None),
            P("dp", None),
            P("dp", None),
            P("dp", None),
            P("dp", None),
            P("dp", None),
        ),
        check_vma=False,
    )
```

profile of v0, /device:TPU:0, one launch (start us, length us, event | category | flops | bytes accessed | tf_op | source)
XLA Modules:
  0.0 649.6 jit_solution(2259845815562270871)
XLA Ops:
  7.2 21.8 %all_gather.22 = bf16[512,64]{1,0:T(8,128)(2,1)S(1)} all-gather(bf16[32,64]{1,0:T(8,128)(2,1)} %param.17), channel_id=1, replica_groups=mesh['dp'=16,'graph'=8] {'dp'}, dimensions={0}, use_global_device_ids=true | all-gather | bytes 69632 | tf_op jit(solution)/shard_map/all_gather | solution.py:32
  29.1 18.8 %all_gather.21 = bf16[512,512]{1,0:T(8,128)(2,1)S(1)} all-gather(bf16[32,512]{1,0:T(8,128)(2,1)} %param.16), channel_id=1, replica_groups=mesh['dp'=16,'graph'=8] {'dp'}, dimensions={0}, use_global_device_ids=true | all-gather | bytes 557056 | tf_op jit(solution)/shard_map/all_gather | solution.py:31
  47.9 2.3 multiply_convert_fusion.6
  50.2 1.0 copy-done.4
  51.2 1.1 fusion.5
  52.3 18.1 %all-gather.1 = bf16[16,4,512]{2,1,0:T(4,128)(2,1)S(1)} all-gather(bf16[1,4,512]{2,1,0:T(4,128)(2,1)S(1)} %bitcast.62), channel_id=1, replica_groups=mesh['dp'=16,'graph'=8] {'dp'}, dimensions={0}, use_global_device_ids=true | all-gather | bytes 69632 | tf_op jit(solution)/shard_map/all_gather | solution.py:34
  70.5 16.2 %all-gather = bf16[16,1,64]{2,1,0:T(2,128)(2,1)S(1)} all-gather(bf16[1,1,64]{2,1,0:T(2,128)(2,1)S(1)} %bitcast.63), channel_id=1, replica_groups=mesh['dp'=16,'graph'=8] {'dp'}, dimensions={0}, use_global_device_ids=true | all-gather | bytes 2176 | tf_op jit(solution)/shard_map/all_gather | solution.py:33
  86.8 21.2 %all_gather.26 = bf16[512,512]{1,0:T(8,128)(2,1)} all-gather(bf16[32,512]{1,0:T(8,128)(2,1)S(1)} %copy-done.19), channel_id=1, replica_groups=mesh['dp'=16,'graph'=8] {'dp'}, dimensions={0}, use_global_device_ids=true | all-gather | bytes 557056 | tf_op jit(solution)/shard_map/all_gather | solution.py:35
  107.9 20.0 %all_gather.27 = bf16[512,512]{1,0:T(8,128)(2,1)} all-gather(bf16[32,512]{1,0:T(8,128)(2,1)S(1)} %copy-done.20), channel_id=1, replica_groups=mesh['dp'=16,'graph'=8] {'dp'}, dimensions={0}, use_global_device_ids=true | all-gather | bytes 557056 | tf_op jit(solution)/shard_map/all_gather | solution.py:36
  127.9 1.8 fusion.19
  129.7 2.0 copy.32
  131.8 29.4 %gather_fusion = bf16[8192,64]{1,0:T(8,128)(2,1)} fusion(bf16[64,8192]{0,1:T(8,128)(2,1)S(1)} %copy.32, s32[8192]{0:T(1024)S(1)} %get-tuple-element.14), kind=kCustom, calls=%fused_computation | custom fusion | bytes 2129920 | tf_op jit(solution)/shard_map/jit(_take)/gather | solution.py:46
  161.2 2.8 copy.33
  164.0 2.8 fusion.2
  166.9 3.8 copy.34
  170.7 44.6 %scatter_custom_fusion = f32[64,1024]{0,1:T(8,128)S(1)} fusion(s32[8192]{0:T(1024)S(1)} %get-tuple-element.13, f32[8192,64]{1,0:T(8,128)} %copy.34, f32[]{:T(128)} %constant.22.clone.1), kind=kCustom, calls=%fused_computation.33 | custom fusion | flops 524288 | bytes 262656 | tf_op jit(solution)/shard_map/scatter-add | solution.py:48
  215.3 0.7 multiply_convert_fusion.5
  216.1 0.5 copy-done.14
  216.6 1.0 multiply_convert_fusion.4
  217.6 0.3 copy-done.24
  217.9 1.3 multiply_convert_fusion.3
  219.2 1.2 multiply_convert_fusion.2
  220.4 1.3 multiply_convert_fusion.1
  221.8 1.0 copy-done.7
  222.7 0.4 convolution_bitcast_fusion.1
  223.4 27.9 %gather_fusion.1 = f32[8192,64]{1,0:T(8,128)} fusion(f32[64,1024]{0,1:T(8,128)S(1)} %copy.35, s32[8192]{0:T(1024)S(1)} %get-tuple-element.12), kind=kCustom, calls=%fused_computation.1 | custom fusion | bytes 4227072 | tf_op jit(solution)/shard_map/jit(_take)/gather | solution.py:64
  251.3 4.0 copy.36
  255.2 3.2 fusion
  258.4 3.9 copy.37
  262.3 46.5 %scatter_custom_fusion.1 = f32[64,8192]{0,1:T(8,128)} fusion(s32[8192]{0:T(1024)S(1)} %get-tuple-element.15, f32[8192,64]{1,0:T(8,128)} %copy.37, f32[]{:T(128)} %constant.22.clone.1), kind=kCustom, calls=%fused_computation.21 | custom fusion | flops 524288 | bytes 2097664 | tf_op jit(solution)/shard_map/scatter-add | solution.py:66
  309.1 0.9 copy-done.8
  310.5 2.3 fusion.27
  312.8 1.2 reshape.72
  314.3 3.0 fusion.26
  317.2 2.6 reshape.71
  319.8 2.3 convolution_bitcast_fusion.2
  322.1 70.0 %reduce-scatter.2.cloned.1.call-done = f32[64,1024]{0,1:T(8,128)} async-done(((f32[64,8192]{0,1:T(8,128)}), f32[64,1024]{0,1:T(8,128)}) %reduce-scatter.2.cloned.1.call-update) | async-done | bytes 262160 | tf_op jit(solution)/shard_map/reduce_scatter | solution.py:67
  392.1 1.9 fusion.12
  394.2 2.4 multiply_convert_fusion
  396.6 1.0 copy-done.26
  397.6 0.7 convolution_bitcast_fusion
  398.3 0.3 copy.38
  398.7 1.2 reshape.68
  399.8 2.4 constant_dynamic-update-slice_fusion.1
  402.2 0.6 constant_dynamic-update-slice_fusion
  402.9 1.3 dynamic-update-slice.2
  404.2 1.8 dynamic-update-slice.3
  406.0 5.0 dynamic-update-slice.4
  411.0 4.5 dynamic-update-slice.5
  415.6 4.7 reshape.73
  420.4 0.6 copy-done.25
  421.0 0.6 dynamic-slice
  422.2 129.2 %all-reduce.6.cloned.1.call-done = f32[852992]{0:T(1024)} async-done(((f32[852992]{0:T(1024)}), f32[852992]{0:T(1024)}) %all-reduce.6.cloned.1.call-update) | async-done | bytes 3411984
  551.5 1.7 dynamic-slice.1
  553.2 1.7 convolution_convert_fusion
  555.0 81.8 %all-reduce.4.cloned.1.call-done = f32[53312]{0:T(1024)} async-done(((f32[53312]{0:T(1024)}), f32[53312]{0:T(1024)}) %all-reduce.4.cloned.1.call-update) | async-done | bytes 213264 | tf_op jit(solution)/shard_map/psum | solution.py:84
  636.8 1.0 fusion.24
  637.9 0.6 reshape.79
  638.5 0.8 fusion.25
  639.3 0.6 reshape.77
  639.9 0.7 reshape.75
  640.6 0.6 reshape.78
  641.2 0.6 reshape.74
  641.9 1.2 slice_bitcast_fusion
  (76 shorter events, 1.8 us)
Async XLA Ops:
  7.2 40.7 %copy-start = (bf16[1024,512]{1,0:T(8,128)(2,1)S(1)}, bf16[1024,512]{1,0:T(8,128)(2,1)}, u32[]{:S(2)}) copy-start(bf16[1024,512]{1,0:T(8,128)(2,1)} %param.11) | copy-start | bytes 3145732
  7.2 122.6 %all-gather.4.cloned.1.call-start = ((), (), s32[]{:S(2)}) async-start(), calls=%async_computation.1 | async-start | bytes 1179648 | tf_op jit(solution)/shard_map/all_gather | solution.py:43
  47.8 2.4 copy-start.12
  47.8 4.5 copy-start.22
  47.8 22.7 %copy-start.23 = (bf16[1,64]{1,0:T(2,128)(2,1)S(1)}, bf16[1,64]{1,0:T(2,128)(2,1)}, u32[]{:S(2)}) copy-start(bf16[1,64]{1,0:T(2,128)(2,1)} %param.18) | copy-start | bytes 388
  47.8 38.9 %copy-start.17 = (s32[8192]{0:T(1024)S(1)}, s32[8192]{0:T(1024)}, u32[]{:S(2)}) copy-start(s32[8192]{0:T(1024)} %param.14) | copy-start | bytes 98308
  47.9 38.8 %copy-start.18 = (s32[8192]{0:T(1024)S(1)}, s32[8192]{0:T(1024)}, u32[]{:S(2)}) copy-start(s32[8192]{0:T(1024)} %param.15) | copy-start | bytes 98308
  47.9 38.9 %copy-start.19 = (bf16[32,512]{1,0:T(8,128)(2,1)S(1)}, bf16[32,512]{1,0:T(8,128)(2,1)}, u32[]{:S(2)}) copy-start(bf16[32,512]{1,0:T(8,128)(2,1)} %param.20) | copy-start | bytes 98308
  50.2 1.0 copy-start.4
  50.2 57.7 %copy-start.20 = (bf16[32,512]{1,0:T(8,128)(2,1)S(1)}, bf16[32,512]{1,0:T(8,128)(2,1)}, u32[]{:S(2)}) copy-start(bf16[32,512]{1,0:T(8,128)(2,1)} %param.21) | copy-start | bytes 98308
  50.2 77.7 %copy-start.16 = (bf16[16,8192]{1,0:T(8,128)(2,1)S(1)}, bf16[16,8192]{1,0:T(8,128)(2,1)}, u32[]{:S(2)}) copy-start(bf16[16,8192]{1,0:T(8,128)(2,1)} %param.13) | copy-start | bytes 786436
  52.3 339.8 %reduce-scatter.2.cloned.1.call-start = ((), (), s32[]{:S(2)}) async-start(), calls=%async_computation.2 | async-start | bytes 4718592 | tf_op jit(solution)/shard_map/reduce_scatter | solution.py:67
  161.2 2.8 copy-start.1
  215.3 0.8 copy-start.9
  215.3 1.2 copy-start.14
  216.1 1.5 copy-start.28
  216.5 1.0 copy-start.15
  216.5 1.4 copy-start.24
  217.6 1.7 copy-start.31
  219.2 1.2 copy-start.32
  220.4 1.3 copy-start.30
  221.7 1.0 copy-start.7
  251.3 4.0 copy-start.2
  308.8 1.2 copy-start.8
  308.8 1.4 copy-start.10
  308.8 242.7 %all-reduce.6.cloned.1.call-start = ((), (), s32[]{:S(2)}) async-start(), calls=%async_computation.4 | async-start | bytes 6823936
  312.8 1.5 copy-start.29
  317.2 2.6 copy-start.3
  392.1 2.0 copy-start.11
  396.6 1.0 copy-start.26
  398.7 4.2 copy-start.21
  398.7 7.3 %copy-start.6 = (f32[16,16384]{1,0:T(8,128)S(1)}, f32[16,16384]{1,0:T(8,128)}, u32[]{:S(2)}) copy-start(f32[16,16384]{1,0:T(8,128)} %reshape.71) | copy-start | bytes 3145732
  399.8 11.2 %copy-start.5 = (f32[16,16384]{1,0:T(8,128)S(1)}, f32[16,16384]{1,0:T(8,128)}, u32[]{:S(2)}) copy-start(f32[16,16384]{1,0:T(8,128)} %reshape.72) | copy-start | bytes 3145732
  420.3 0.7 copy-start.25
  420.3 132.9 %copy-start.13 = (bf16[512,512]{1,0:T(8,128)(2,1)S(1)}, bf16[512,512]{1,0:T(8,128)(2,1)}, u32[]{:S(2)}) copy-start(bf16[512,512]{1,0:T(8,128)(2,1)} %copy-done.12) | copy-start | bytes 1572868
  420.3 132.9 %copy-start.27 = (bf16[1024,512]{1,0:T(8,128)(2,1)S(1)}, bf16[1024,512]{1,0:T(8,128)(2,1)}, u32[]{:S(2)}) copy-start(bf16[1024,512]{1,0:T(8,128)(2,1)} %copy-done.26) | copy-start | bytes 3145732
  420.4 216.5 %all-reduce.4.cloned.1.call-start = ((), (), s32[]{:S(2)}) async-start(), calls=%async_computation.3 | async-start | bytes 434176 | tf_op jit(solution)/shard_map/psum | solution.py:84
Sparse Core Ops, SparseCore 0:
  52.4 45.3 all-gather.3
  308.9 83.1 reduce-scatter.1
  420.5 130.9 all-reduce.5
  553.9 82.8 all-reduce.3
where the time goes:
time: 651 us; the launch traced here: 650 us
  waiting for transfers between devices  281 us (43%)
  blocking collectives  116 us (18%)
  local copies, waits for them, and re-layouts  114 us (18%)
  other arithmetic  97.2 us (15%)
  matrix products  25.8 us (4%)
  between operations  14.8 us (2%)
    unnamed x5, waiting for transfers between devices  129 us
    psum x1, waiting for transfers between devices, on_device(): shares = lax.psum(rows_sum, 'graph')  81.8 us
    reduce_scatter x1, waiting for transfers between devices, on_device(): lax.psum_scatter(partial_down, 'graph', scatter_dimension=1, tiled=True)  70 us
    scatter-add x1, other arithmetic, on_device(): jnp.zeros((width_trip, group_cols), f32).at[:, source_edge]  46.5 us
    scatter-add x1, other arithmetic, on_device(): jnp.zeros((width_trip, edge_rows), f32).at[:, target_edge]  44.6 us
    gather x2, local copies, waits for them, and re-layouts, on_device(): down_in = jnp.take(group_down, source_edge, axis=1).astype(f32)  32.3 us
    gather x2, local copies, waits for them, and re-layouts, on_device(): dagg_out = jnp.take(dagg_t, target_edge, axis=1)  31.8 us
    all_gather x1, blocking collectives, on_device(): lax.all_gather(down_weight, 'dp', axis=0, tiled=True)  21.8 us
  transfers between devices with their start and end apart: 4, of which 3 were waited for; matrix products, arithmetic and copies ran while one was open for 2% of the time, Pallas kernels for 0%

commit v1 on v0

v1 whole, which is shorter than its diff:
```python
import functools
import math

import jax
import jax.numpy as jnp
from jax import lax
from jax.experimental import pallas as pl
from jax.experimental.pallas import tpu as pltpu
from jax.sharding import PartitionSpec as P

F32 = jnp.float32
BF16 = jnp.bfloat16
SCALE = math.sqrt(0.5)
NT = (((1,), (1,)), ((), ()))
TN = (((0,), (0,)), ((), ()))
LANES = 128
SMALL_ROWS = 16
CHUNK = 256
GROUP = 20
LINES = 16
PIECE = 512
MIB = 1024 * 1024


def dot(a, b, dims=(((1,), (0,)), ((), ()))):
    return lax.dot_general(a, b, dims, preferred_element_type=F32)


def silu_and_slope(value):
    sig = jax.nn.sigmoid(value)
    return value * sig, sig * (1.0 + value * (1.0 - sig))


def iota(shape, dim):
    return lax.broadcasted_iota(jnp.int32, shape, dim)


def one_hot(index_row, rows):
    hit = iota((rows, index_row.shape[1]), 0) == index_row
    return jnp.where(hit, 1.0, 0.0).astype(BF16)


def spread(value, part_row, parts):
    return jnp.concatenate(
        [jnp.where(part_row == part, value, 0.0) for part in range(parts)], axis=0
    ).astype(BF16)


def pick(stack, part_row, parts):
    width = stack.shape[0] // parts
    total = stack[:width]
    for part in range(1, parts):
        total = jnp.where(part_row == part, stack[part * width : (part + 1) * width], total)
    return total


def call(kernel, out_shape, *operands, scratch=(), vmem=32, smem=(), hbm=(), lazy=()):
    fetched = tuple(hbm) + tuple(lazy)

    def body(*refs):
        refs = list(refs)
        sems = refs.pop()
        places = refs[len(refs) - len(fetched) :]
        refs = refs[: len(refs) - len(fetched)]
        copies = []
        for k, (operand, place) in enumerate(zip(fetched, places)):
            copies.append(pltpu.make_async_copy(refs[operand], place, sems.at[k]))
            copies[-1].start()
            refs[operand] = place
        for copy in copies[: len(hbm)]:
            copy.wait()

        def ready():
            for copy in copies[len(hbm) :]:
                copy.wait()

        if lazy:
            kernel(ready, *refs)
        else:
            kernel(*refs)

    def space(k):
        return pltpu.SMEM if k in smem else pltpu.HBM if k in fetched else pltpu.VMEM

    return pl.pallas_call(
        body if fetched else kernel,
        out_shape=out_shape,
        in_specs=[pl.BlockSpec(memory_space=space(k)) for k in range(len(operands))],
        out_specs=jax.tree.map(lambda _: pl.BlockSpec(memory_space=pltpu.VMEM), out_shape),
        scratch_shapes=list(scratch)
        + [pltpu.VMEM(operands[k].shape, operands[k].dtype) for k in fetched]
        + [pltpu.SemaphoreType.DMA((len(fetched),))] * bool(fetched),
        compiler_params=pltpu.CompilerParams(vmem_limit_bytes=vmem * MIB),
    )(*operands)


def order_kernel(peers, e_dev, source_ref, target_ref, basis_ref, rows_ref, sorted_ref, owner_ref, pos, acc):
    lines, lanes = source_ref.shape
    source = source_ref[...]
    peer = source // e_dev
    hits = jnp.concatenate(
        [jnp.where(peer == p, 1.0, 0.0) for p in range(peers)], axis=0
    ).astype(BF16)
    full = peers * lines
    row, col = iota((lanes, lanes), 0), iota((lanes, lanes), 1)
    before = dot(hits, jnp.where(row < col, 1.0, 0.0).astype(BF16))
    count = dot(hits, jnp.ones((lanes, LANES), BF16)).astype(BF16)
    row, col = iota((full, full), 0), iota((full, full), 1)
    same = row // lines == col // lines
    line_start = dot(jnp.where(same & (col < row), 1.0, 0.0).astype(BF16), count)
    in_peer = dot(jnp.where(same, 1.0, 0.0).astype(BF16), count)
    chunks = (in_peer.astype(jnp.int32) + (CHUNK - 1)) // CHUNK
    first_line = (col // lines < row // lines) & (col % lines == 0)
    first_chunk = dot(
        jnp.where(first_line, 1.0, 0.0).astype(BF16), chunks.astype(F32).astype(BF16)
    ).astype(jnp.int32)
    at = iota((1, LANES), 1)
    owner = jnp.zeros((1, LANES), jnp.int32)
    start = (first_chunk * CHUNK).astype(F32) + line_start
    total = jnp.zeros((lines, lanes), F32)
    for p in range(peers):
        block = slice(p * lines, (p + 1) * lines)
        wide = jnp.concatenate([start[block]] * (lanes // LANES), axis=1)
        total = jnp.where(peer == p, wide + before[block], total)
        if p > 0:
            owner += jnp.where(first_chunk[p * lines : p * lines + 1, :] <= at, 1, 0)
    owner_ref[...] = owner
    pos[...] = total.astype(jnp.int32)

    width = LINES * lanes
    pieces = sorted_ref.shape[1] // PIECE
    nb = basis_ref.shape[0]
    extra = 8

    def line(ref, step):
        return jnp.concatenate(
            [ref[pl.ds(step * LINES + k, 1), :] for k in range(LINES)], axis=1
        )

    acc[...] = jnp.zeros_like(acc)

    def place(step, carry):
        here = line(pos, step)
        src = line(source_ref, step) & (e_dev - 1)
        tgt = line(target_ref, step)
        cols = pl.ds(pl.multiple_of(step * width, width), width)
        index = jnp.concatenate(
            [src % CHUNK, src // CHUNK, tgt % CHUNK, tgt // CHUNK]
            + [jnp.zeros((extra - 4, width), jnp.int32)],
            axis=0,
        )
        value = jnp.concatenate([basis_ref[:, cols].astype(F32), index.astype(F32)], axis=0)
        acc[...] += dot(spread(value, here // PIECE, pieces), one_hot(here % PIECE, PIECE), NT)
        return carry

    lax.fori_loop(0, lines // LINES, place, 0)
    for piece in range(pieces):
        cols = slice(piece * PIECE, (piece + 1) * PIECE)
        base = piece * (nb + extra)
        sorted_ref[:, cols] = acc[base : base + nb, :].astype(BF16)
        rows_ref[:, cols] = acc[base + nb : base + nb + extra, :].astype(jnp.int32)


def forward_kernel(
    ready,
    owner_ref,
    core_ref,
    down_ref,
    rows_ref,
    basis_ref,
    w_basis_ref,
    w_up_ref,
    w_first_ref,
    w_second_ref,
    cot_ref,
    early_ref,
    early_other_ref,
    up_grad_ref,
    dagg_ref,
    down_in_ref,
    second_s,
    first_s,
    agg_acc,
    agg_s,
    mixed_s,
    inner_s,
    dz_four_s,
    dz_three_s,
    dz_two_s,
):
    peers, stack_rows, e_hi = down_ref.shape
    slots = rows_ref.shape[1]
    trip = w_up_ref.shape[0]
    parts = stack_rows // trip
    width = GROUP * CHUNK
    agg_acc[...] = jnp.zeros_like(agg_acc)

    def forward(step, carry):
        cols = pl.ds(pl.multiple_of(step * width, width), width)
        found = []
        for k in range(GROUP):
            here = pl.ds(pl.multiple_of(step * width + k * CHUNK, CHUNK), CHUNK)
            owner = owner_ref[0, step * GROUP + k]
            hot = one_hot(rows_ref[0:1, here], e_hi)
            found.append(pick(dot(down_ref[owner], hot), rows_ref[1:2, here], parts))
        down_in = jnp.concatenate(found, axis=1)
        coeff = dot(w_basis_ref[...], basis_ref[:, cols])
        down_in_ref[:, cols] = down_in.astype(BF16)
        hot_e = one_hot(rows_ref[2:3, cols], e_hi)
        placed = spread(down_in * coeff, rows_ref[3:4, cols], parts)
        agg_acc[...] += dot(hot_e, placed, NT)
        return carry

    lax.fori_loop(0, slots // width, forward, 0)

    ready()
    w_up = w_up_ref[...]
    w_first = w_first_ref[...]
    w_second = w_second_ref[...]
    for q in range(parts):
        rows = slice(q * e_hi, (q + 1) * e_hi)
        agg = agg_acc[:, q * trip : (q + 1) * trip].astype(BF16)
        agg_s[rows, :] = agg
        act, slope_two = silu_and_slope(dot(agg, w_up))
        mixed = act.astype(BF16)
        mixed_s[rows, :] = mixed
        act, slope_three = silu_and_slope(dot(mixed, w_first))
        inner = act.astype(BF16)
        inner_s[rows, :] = inner
        slope_four = silu_and_slope(dot(inner, w_second))[1]
        cot = SCALE * cot_ref[rows, :].astype(F32)
        dz_four = (cot * slope_four).astype(BF16)
        dz_four_s[rows, :] = dz_four
        dz_three = (dot(dz_four, w_second, NT) * slope_three).astype(BF16)
        dz_three_s[rows, :] = dz_three
        dz_two = ((cot + dot(dz_three, w_first, NT)) * slope_two).astype(BF16)
        dz_two_s[rows, :] = dz_two
        dagg_ref[q * trip : (q + 1) * trip, :] = dot(w_up, dz_two, NT).astype(BF16)

    second_s[...] = dot(inner_s[...], dz_four_s[...], TN).astype(BF16)
    first_s[...] = dot(mixed_s[...], dz_three_s[...], TN).astype(BF16)
    up_grad_ref[...] = dot(agg_s[...], dz_two_s[...], TN)
    pairs = early_ref.shape[0]
    share = w_first.shape[0] // (2 * pairs)
    core = core_ref[0]
    for pair in range(pairs):
        for ref, side in ((early_ref, core), (early_other_ref, 1 - core)):
            at = pl.ds(pl.multiple_of((2 * pair + side) * share, share), share)
            ref[pair, :share, :] = second_s[at, :]
            ref[pair, share:, :] = first_s[at, :]


def backward_kernel(
    owner_ref, dagg_ref, rows_ref, basis_ref, w_basis_ref, down_in_ref, partial_ref, basis_grad, total
):
    peers, stack_rows, e_hi = partial_ref.shape
    slots = rows_ref.shape[1]
    trip = w_basis_ref.shape[0]
    parts = stack_rows // trip
    width = GROUP * CHUNK
    basis_grad[...] = jnp.zeros_like(basis_grad)
    total[...] = jnp.zeros_like(total)

    def backward(step, carry):
        cols = pl.ds(pl.multiple_of(step * width, width), width)
        hot_e = one_hot(rows_ref[2:3, cols], e_hi)
        dagg_out = pick(dot(dagg_ref[...], hot_e), rows_ref[3:4, cols], parts)
        dcoeff = (dagg_out * down_in_ref[:, cols].astype(F32)).astype(BF16)
        basis_grad[...] += dot(basis_ref[:, cols], dcoeff, NT)
        coeff = dot(w_basis_ref[...], basis_ref[:, cols])
        placed = spread(dagg_out * coeff, rows_ref[1:2, cols], parts)
        hot = one_hot(rows_ref[0:1, cols], e_hi)
        terms = []
        for k in range(GROUP):
            here = slice(k * CHUNK, (k + 1) * CHUNK)
            terms.append(dot(placed[:, here], hot[:, here], NT))
        for k in range(GROUP):
            total[owner_ref[0, step * GROUP + k]] += terms[k]
        return carry

    lax.fori_loop(0, slots // width, backward, 0)
    partial_ref[...] = total[...].astype(BF16)


def order(source, target, basis, peers, e_dev):
    shape = jax.ShapeDtypeStruct
    trips = source.shape[0]
    slots = trips + peers * CHUNK
    nb = basis.shape[0]
    lines = trips // LANES
    return call(
        functools.partial(order_kernel, peers, e_dev),
        (shape((8, slots), jnp.int32), shape((nb, slots), BF16), shape((1, LANES), jnp.int32)),
        source.reshape(lines, LANES),
        target.reshape(lines, LANES),
        basis,
        scratch=[
            pltpu.VMEM((lines, LANES), jnp.int32),
            pltpu.VMEM((slots // PIECE * (nb + 8), PIECE), F32),
        ],
        hbm=(0, 1, 2),
        vmem=60,
    )


def forward(owner, core, down, rows, basis, w_basis_t, w_up, w_first, w_second, cot):
    shape = jax.ShapeDtypeStruct
    vmem = pltpu.VMEM
    edges, width = cot.shape
    trip = w_up.shape[0]
    nb = basis.shape[0]
    slots = rows.shape[1]
    return call(
        forward_kernel,
        (
            shape((nb // 2, 2 * width // nb, width), BF16),
            shape((nb // 2, 2 * width // nb, width), BF16),
            shape((trip, width), F32),
            shape((edges // CHUNK * trip, CHUNK), BF16),
            shape((trip, slots), BF16),
        ),
        owner,
        core,
        down,
        rows,
        basis,
        w_basis_t,
        w_up,
        w_first,
        w_second,
        cot,
        scratch=[
            vmem((width, width), BF16),
            vmem((width, width), BF16),
            vmem((CHUNK, edges // CHUNK * trip), F32),
            vmem((edges, trip), BF16),
        ]
        + [vmem((edges, width), BF16)] * 5,
        smem=(0, 1),
        hbm=(2, 3, 4, 5),
        lazy=(6, 7, 8, 9),
        vmem=60,
    )


def backward(owner, dagg, rows, basis, w_basis_t, down_in, peers):
    shape = jax.ShapeDtypeStruct
    nb = basis.shape[0]
    trip = w_basis_t.shape[0]
    stack = (peers,) + dagg.shape
    return call(
        backward_kernel,
        (shape(stack, BF16), shape((nb, trip), F32)),
        owner,
        dagg,
        rows,
        basis,
        w_basis_t,
        down_in,
        scratch=[pltpu.VMEM(stack, F32)],
        smem=(0,),
        hbm=(2, 3),
        vmem=40,
    )


def pack_kernel(pair_ref, down_ref, basis_ref, up_ref, first_ref, second_ref, out_ref, small):
    small[...] = jnp.zeros_like(small)
    share = pair_ref.shape[0]
    trip = down_ref.shape[1]
    up_rows = up_ref.shape[0]
    small[:up_rows, :] = up_ref[...].astype(F32)
    small[up_rows : up_rows + 1, :trip] = basis_ref[...].astype(F32)
    place_down(small, down_ref[...].astype(F32))
    rest = small[...].astype(BF16)
    for partner in range(out_ref.shape[0]):
        out_ref[partner, :share, :] = pair_ref[...]
        out_ref[partner, share : 2 * share, :] = second_ref[...]
        out_ref[partner, 2 * share : 3 * share, :] = first_ref[...]
        out_ref[partner, 3 * share :, :] = rest


def place_down(small, down):
    for group in range(down.shape[0] // 8):
        small[8:16, group * LANES : group * LANES + down.shape[1]] = down[
            group * 8 : (group + 1) * 8, :
        ]


def take_down(small, rows, trip):
    return [
        small[8:16, group * LANES : group * LANES + trip] for group in range(rows // 8)
    ]


def down_kernel(core_ref, feats_ref, own_ref, other_ref, down_ref, head_ref):
    rows, width = feats_ref.shape
    peers, stack_rows, block = down_ref.shape
    trip = stack_rows * block // rows
    pairs = own_ref.shape[0]
    share = width // (2 * pairs)
    core = core_ref[0]
    for pair in range(pairs):
        for ref, side in ((own_ref, core), (other_ref, 1 - core)):
            at = pl.ds(pl.multiple_of((2 * pair + side) * share, share), share)
            head_ref[at, :width] = ref[pair, :share, :]
            small = ref[pair, 3 * share :, :].astype(F32)
            down = jnp.concatenate(take_down(small, share, LANES), axis=0)
            head_ref[at, width:] = down.astype(BF16)
    w_pair = head_ref[:, :width]
    w_down = head_ref[:, width : width + trip]
    for part in range(rows // block):
        z_one = dot(feats_ref[part * block : (part + 1) * block, :], w_pair)
        hidden = silu_and_slope(z_one)[0].astype(BF16)
        down_t = dot(hidden, w_down).T.astype(BF16)
        for peer in range(peers):
            down_ref[peer, part * trip : (part + 1) * trip, :] = down_t


def hidden_kernel(
    core_ref,
    feats_ref,
    weights_ref,
    own_ref,
    other_ref,
    hidden_ref,
    slope_ref,
    second_ref,
    first_ref,
    up_ref,
    basis_ref,
    up_s,
    basis_s,
):
    rows, width = feats_ref.shape
    pairs = own_ref.shape[0]
    share = width // (2 * pairs)
    up_rows = up_ref.shape[0] // (2 * pairs)
    trip = basis_ref.shape[0]
    core = core_ref[0]
    for pair in range(pairs):
        for ref, side in ((own_ref, core), (other_ref, 1 - core)):
            at = pl.ds(pl.multiple_of((2 * pair + side) * share, share), share)
            second_ref[at, :] = ref[pair, share : 2 * share, :]
            first_ref[at, :] = ref[pair, 2 * share : 3 * share, :]
            small = ref[pair, 3 * share :, :].astype(F32)
            up_s[2 * pair + side] = small[:up_rows]
            basis_s[2 * pair + side] = small[up_rows : up_rows + 1, :LANES]
    up_ref[...] = jnp.concatenate([up_s[k] for k in range(2 * pairs)], axis=0).astype(BF16)
    basis = jnp.concatenate([basis_s[k] for k in range(2 * pairs)], axis=0)
    basis_ref[...] = basis.T[:trip].astype(BF16)
    w_pair = weights_ref[:, :width]
    for first in range(0, rows, CHUNK):
        block = slice(first, first + CHUNK)
        act, slope = silu_and_slope(dot(feats_ref[block, :], w_pair))
        hidden_ref[block, :] = act.astype(BF16)
        slope_ref[block, :] = slope.astype(BF16)


def tail_kernel(
    core_ref,
    parts_ref,
    hidden_ref,
    slope_ref,
    feats_ref,
    weights_ref,
    basis_ref,
    up_ref,
    early_ref,
    early_other_ref,
    dz_ref,
    mine_ref,
    theirs_ref,
    ddown_s,
    pair_s,
    small,
):
    peers = parts_ref.shape[0]
    rows, width = feats_ref.shape
    trip = ddown_s.shape[1]
    summed = parts_ref[0].astype(F32)
    for peer in range(1, peers):
        summed += parts_ref[peer].astype(F32)
    span = summed.shape[1]
    for part in range(rows // span):
        ddown_s[part * span : (part + 1) * span, :] = summed[
            part * trip : (part + 1) * trip, :
        ].T.astype(BF16)
    w_down = weights_ref[:, width : width + trip]
    for first in range(0, rows, 256):
        block = slice(first, first + 256)
        dz_ref[block, :] = (
            dot(ddown_s[block, :], w_down, NT) * slope_ref[block, :].astype(F32)
        ).astype(BF16)
    down = dot(hidden_ref[...], ddown_s[...], TN)
    pair_s[...] = dot(feats_ref[...], dz_ref[...], TN).astype(BF16)
    owners = basis_ref.shape[0]
    share = width // owners
    up_rows = trip // owners
    small[...] = jnp.zeros_like(small)
    for owner in range(owners):
        small[owner, :up_rows, :] = up_ref[owner * up_rows : (owner + 1) * up_rows, :]
        small[owner, up_rows : up_rows + 1, :trip] = basis_ref[owner : owner + 1, :]
        place_down(small.at[owner], down[owner * share : (owner + 1) * share])
    core = core_ref[0]
    for pair in range(owners // 2):
        for ref, side, half in (
            (mine_ref, core, early_ref),
            (theirs_ref, 1 - core, early_other_ref),
        ):
            owner = 2 * pair + side
            at = pl.ds(pl.multiple_of(owner * share, share), share)
            ref[pair, :share, :] = pair_s[at, :]
            ref[pair, share : share + SMALL_ROWS, :] = small[owner].astype(BF16)
            ref[pair, share + SMALL_ROWS :, :] = half[pair]


def edge_kernel(dz_ref, weights_ref, out_ref):
    out_ref[...] = dot(dz_ref[...], weights_ref[:, : dz_ref.shape[1]], NT).astype(BF16)


def chip_sum_kernel(own_ref, other_ref, out_ref):
    for pair in range(own_ref.shape[0]):
        total = own_ref[pair].astype(F32) + other_ref[pair].astype(F32)
        out_ref[pair] = total.astype(BF16)


def owners_sum_kernel(parts_ref, out_ref):
    total = parts_ref[0].astype(F32)
    for owner in range(1, parts_ref.shape[0]):
        total += parts_ref[owner].astype(F32)
    total = total.astype(BF16)
    for peer in range(out_ref.shape[0]):
        out_ref[peer] = total


def peers_sum_kernel(parts_ref, pair_ref, down_ref, basis_ref, up_ref, first_ref, second_ref):
    share = pair_ref.shape[0]
    trip = down_ref.shape[1]
    up_rows = up_ref.shape[0]
    total = parts_ref[0].astype(F32)
    for peer in range(1, parts_ref.shape[0]):
        total += parts_ref[peer].astype(F32)
    pair_ref[...] = total[:share]
    small = total[share : share + SMALL_ROWS]
    second_ref[...] = total[share + SMALL_ROWS : 2 * share + SMALL_ROWS]
    first_ref[...] = total[2 * share + SMALL_ROWS :]
    up_ref[...] = small[:up_rows]
    basis_ref[...] = small[up_rows : up_rows + 1, :trip]
    for group, rows in enumerate(take_down(small, share, trip)):
        down_ref[group * 8 : (group + 1) * 8, :] = rows


def on_device(
    edge_feats,
    cotangent,
    angle_basis,
    source_edge,
    target_edge,
    pair_weight,
    down_weight,
    basis_weight,
    up_weight,
    res_first,
    res_second,
):
    shape = jax.ShapeDtypeStruct
    vmem = pltpu.VMEM
    owners = lax.axis_size("dp")
    peers = lax.axis_size("graph")
    pairs = owners // 2
    rows, width = edge_feats.shape
    share = pair_weight.shape[0]
    trip = down_weight.shape[1]
    up_rows = up_weight.shape[0]
    nb = angle_basis.shape[0]
    core = (lax.axis_index("dp") % 2).reshape(1)
    same_core = [[2 * pair + side for pair in range(pairs)] for side in range(2)]

    def swap(value):
        return lax.ppermute(value, "dp", [(owner, owner ^ 1) for owner in range(owners)])

    shards = (pair_weight, down_weight, basis_weight, up_weight, res_first, res_second)
    own = call(
        pack_kernel,
        shape((pairs, 3 * share + SMALL_ROWS, width), BF16),
        pair_weight,
        down_weight,
        basis_weight,
        up_weight,
        res_first,
        res_second,
        scratch=[vmem((SMALL_ROWS, width), F32)],
        hbm=range(6),
        vmem=60,
    )
    own = lax.all_to_all(own, "dp", 0, 0, axis_index_groups=same_core)
    other = swap(own)
    index, basis, owner = order(source_edge, target_edge, angle_basis, peers, rows)
    down, head = call(
        down_kernel,
        (
            shape((peers, rows // CHUNK * trip, CHUNK), BF16),
            shape((width, width + LANES), BF16),
        ),
        core,
        edge_feats,
        own,
        other,
        smem=(0,),
        vmem=16,
    )
    down = lax.all_to_all(down, "graph", 0, 0)
    hidden, slope, w_second, w_first, w_up, w_basis_t = call(
        hidden_kernel,
        (
            shape((rows, width), BF16),
            shape((rows, width), BF16),
            shape((width, width), BF16),
            shape((width, width), BF16),
            shape((trip, width), BF16),
            shape((trip, nb), BF16),
        ),
        core,
        edge_feats,
        head,
        own,
        other,
        scratch=[vmem((owners, up_rows, width), F32), vmem((owners, 1, LANES), F32)],
        smem=(0,),
        hbm=(1, 2, 3, 4),
        vmem=60,
    )
    early, early_other, up_grad, dagg, down_in = forward(
        owner, core, down, index, basis, w_basis_t, w_up, w_first, w_second, cotangent
    )
    partial, basis_grad = backward(owner, dagg, index, basis, w_basis_t, down_in, peers)
    parts = lax.all_to_all(partial, "graph", 0, 0)
    half = shape((pairs, 3 * share + SMALL_ROWS, width), BF16)
    dz_one, grads, other = call(
        tail_kernel,
        (shape((rows, width), BF16), half, half),
        core,
        parts,
        hidden,
        slope,
        edge_feats,
        head,
        basis_grad,
        up_grad,
        early,
        early_other,
        scratch=[
            vmem((rows, trip), BF16),
            vmem((width, width), BF16),
            vmem((owners, SMALL_ROWS, width), F32),
        ],
        smem=(0,),
        hbm=(2, 3, 4, 5, 8, 9),
        vmem=32,
    )
    other = swap(other)
    edge_grad = call(edge_kernel, shape((rows, width), BF16), dz_one, head, vmem=16)
    other, edge_grad = lax.optimization_barrier((other, edge_grad))
    chip = call(chip_sum_kernel, half, grads, other, vmem=16)
    chip = lax.all_to_all(chip, "dp", 0, 0, axis_index_groups=same_core)
    sums = call(
        owners_sum_kernel,
        shape((peers, 3 * share + SMALL_ROWS, width), BF16),
        chip,
        vmem=16,
    )
    sums = lax.all_to_all(sums, "graph", 0, 0)
    pair, down_grad, basis_grad, up, first, second = call(
        peers_sum_kernel,
        (
            shape((share, width), F32),
            shape((share, trip), F32),
            shape((1, trip), F32),
            shape((up_rows, width), F32),
            shape((share, width), F32),
            shape((share, width), F32),
        ),
        sums,
        vmem=16,
    )
    return edge_grad, pair, down_grad, basis_grad, up, first, second


def solution(mesh):
    split = P(("dp", "graph"), None)
    line = P(("dp", "graph"))
    rows = P("dp", None)
    return jax.shard_map(
        on_device,
        mesh=mesh,
        in_specs=(split, split, P(None, ("dp", "graph")), line, line) + (rows,) * 6,
        out_specs=(split,) + (rows,) * 6,
        check_vma=False,
    )
```

time: 651 us -> 143 us (0.22)
  waiting for transfers between devices: 281 us -> 8.26 us
  local copies, waits for them, and re-layouts: 114 us -> 7.11 us
  other arithmetic: 97.2 us -> 0 us
  Pallas kernels: 0 us -> 43.5 us
  blocking collectives: 116 us -> 76.1 us
  matrix products: 25.8 us -> 0 us
  between operations: 14.8 us -> 0.84 us
    unnamed x5 -> x0, waiting for transfers between devices: 129 us -> none
    all_gather x6 -> x0, blocking collectives: 116 us -> none  [the longest x1 21.8 us: on_device(): lax.all_gather(down_weight, 'dp', axis=0, tiled=True)]
    scatter-add x2 -> x0, other arithmetic: 91.1 us -> none  [the longest x1 46.5 us: on_device(): jnp.zeros((width_trip, group_cols), f32).at[:, source_edge]]
    psum x1 -> x0, waiting for transfers between devices: 81.8 us -> none  [on_device(): shares = lax.psum(rows_sum, 'graph')]
    all_to_all x0 -> x4, blocking collectives: none -> 76.1 us  [the longest x1 20.7 us: on_device(): own = lax.all_to_all(own, 'dp', 0, 0, axis_index_groups=same_core)]
    reduce_scatter x1 -> x0, waiting for transfers between devices: 70 us -> none  [on_device(): lax.psum_scatter(partial_down, 'graph', scatter_dimension=1, tiled=True)]
    gather x4 -> x0, local copies, waits for them, and re-layouts: 64.1 us -> none  [the longest x2 32.3 us: on_device(): down_in = jnp.take(group_down, source_edge, axis=1).astype(f32)]
    pallas_call x0 -> x11, Pallas kernels: none -> 43.5 us  [call(): pl.pallas_call(body if fetched else kernel, out_shape=out_shape, in_specs...]
  transfers between devices with their start and end apart: 4 -> 3, of which waited for: 3 -> 3; matrix products, arithmetic and copies ran while one was open for 2% -> 0% of each run, Pallas kernels for 0% -> 10%
where the time goes in v1:
time: 143 us
  blocking collectives  76.1 us (53%)
  Pallas kernels  43.5 us (30%)
  waiting for transfers between devices  8.26 us (6%)
  local copies, waits for them, and re-layouts  7.11 us (5%)
  starting transfers between devices  6.72 us (5%)
    pallas_call x11, Pallas kernels, call(): pl.pallas_call(body if fetched else kernel, out_shape=out_shape, in_specs...  43.5 us
    all_to_all x1, blocking collectives, on_device(): own = lax.all_to_all(own, 'dp', 0, 0, axis_index_groups=same_core)  20.7 us
    all_to_all x1, blocking collectives, on_device(): parts = lax.all_to_all(partial, 'graph', 0, 0)  20 us
    all_to_all x1, blocking collectives, on_device(): sums = lax.all_to_all(sums, 'graph', 0, 0)  18 us
    all_to_all x1, blocking collectives, on_device(): chip = lax.all_to_all(chip, 'dp', 0, 0, axis_index_groups=same_core)  17.4 us
    unnamed x38, local copies, waits for them, and re-layouts  7.11 us
    all_to_all x1, starting transfers between devices, on_device(): down = lax.all_to_all(down, 'graph', 0, 0)  6.64 us
    all_to_all x1, waiting for transfers between devices, on_device(): down = lax.all_to_all(down, 'graph', 0, 0)  5.04 us
  transfers between devices with their start and end apart: 3, of which 3 were waited for; matrix products, arithmetic and copies ran while one was open for 0% of the time, Pallas kernels for 10%

profile of v1, /device:TPU:0, one launch (start us, length us, event | category | flops | bytes accessed | tf_op | source)
XLA Modules:
  0.0 142.5 jit_solution(10048247984869077624)
XLA Ops:
  0.6 0.0 copy-start
  0.6 2.0 %shard_map.163 = bf16[8,112,512]{2,1,0:T(8,128)(2,1)} custom-call(bf16[32,512]{1,0:T(8,128)(2,1)} %refs_0_.1, bf16[32,64]{1,0:T(8,128)(2,1)} %refs_1_.2, bf16[1,64]{1,0:T(2,128)(2,1)} %refs_2_.3, bf16[4,512]{1,0:T(4,128)(2,1)} %refs_3_.1, bf16[32,512]{1,0:T(8,128)(2,1)} %refs_4_.2, bf16[32,512]{1,0:T(8,128)(2,1)} %refs_5_.1), custom_call_target="tpu_custom_call" | custom-call | tf_op jit(solution)/shard_map/pallas_call | solution.py:85
  2.6 20.7 %all_to_all.25.own_ref.refs_3_ = bf16[8,112,512]{2,1,0:T(8,128)(2,1)S(1)} all-to-all(bf16[8,112,512]{2,1,0:T(8,128)(2,1)} %shard_map.163), channel_id=1, replica_groups={{0,16,32,48,64,80,96,112},{8,24,40,56,72,88,104,120},{1,17,33,49,65,81,..., dimensions={0} | all-to-all | bytes 1835008 | tf_op jit(solution)/shard_map/all_to_all | solution.py:597
  23.4 0.0 copy-start.2
  23.4 0.0 collective-permute-start
  23.4 2.5 %collective-permute-done.other_ref.refs_4_ = bf16[8,112,512]{2,1,0:T(8,128)(2,1)S(1)} collective-permute-done((bf16[8,112,512]{2,1,0:T(8,128)(2,1)S(1)}, bf16[8,112,512]{2,1,0:T(8,128)(2,1)S(1)}, u32[]{:S(2)}, u32[]{:S(2)}) %collective-permute-start) | collective-permute-done | bytes 917536 | tf_op jit(solution)/shard_map/ppermute | solution.py:581
  25.8 0.0 copy-start.5
  25.8 0.0 copy-done
  25.8 1.4 %shard_map.164 = (bf16[8,256,256]{2,1,0:T(8,128)(2,1)S(1)}, bf16[512,640]{1,0:T(8,128)(2,1)S(1)}) custom-call(s32[1]{0:T(128)} %bitcast.core_ref.refs_0_.refs_1_, bf16[1024,512]{1,0:T(8,128)(2,1)S(1)} %copy-done, bf16[8,112,512]{2,1,0:T(8,128)(2,1)S(1)} %all_to_all.25.own_ref.refs_3_, bf16[8,112,512]{2,1,0:T(8,128)(2,1)S(1)} %collective-permute-done.other_ref.refs_4_), custom_call_target="tpu_custom_call" | custom-call | tf_op jit(solution)/shard_map/pallas_call | solution.py:85
  27.3 0.0 copy-done.2
  27.3 0.0 copy-done.5
  27.3 0.0 copy-start.3
  27.3 0.8 copy-done.3
  28.1 0.0 copy-start.9
  28.2 1.0 copy-done.9
  29.1 6.6 %all-to-all-start.1 = ((bf16[8,256,256]{2,1,0:T(8,128)(2,1)}), bf16[8,256,256]{2,1,0:T(8,128)(2,1)S(1)}, u32[]{:S(2)}, u32[]{:S(2)}) async-start(bf16[8,256,256]{2,1,0:T(8,128)(2,1)} %copy-done.9), calls=%async_computation.1 | async-start | bytes 2097152 | tf_op jit(solution)/shard_map/all_to_all | solution.py:613
  35.8 8.0 %shard_map.162 = (s32[8,10240]{1,0:T(8,128)}, bf16[16,10240]{1,0:T(8,128)(2,1)}, s32[1,128]{1,0:T(1,128)}) custom-call(s32[64,128]{1,0:T(8,128)} %bitcast.3, s32[64,128]{1,0:T(8,128)} %bitcast.4, bf16[16,8192]{1,0:T(8,128)(2,1)} %refs_2_.2), custom_call_target="tpu_custom_call" | custom-call | tf_op jit(solution)/shard_map/pallas_call | solution.py:85
  43.7 4.5 %shard_map.165 = (bf16[1024,512]{1,0:T(8,128)(2,1)}, bf16[1024,512]{1,0:T(8,128)(2,1)}, bf16[512,512]{1,0:T(8,128)(2,1)}, bf16[512,512]{1,0:T(8,128)(2,1)}, bf16...) custom-call(s32[1]{0:T(128)} %bitcast.core_ref.refs_0_.refs_1_, bf16[1024,512]{1,0:T(8,128)(2,1)} %refs_4_.3, ...), custom_call_target="tpu_custom_call" | custom-call | tf_op jit(solution)/shard_map/pallas_call | solution.py:85
  48.3 5.0 %all-to-all-done.1.refs_2_ = bf16[8,256,256]{2,1,0:T(8,128)(2,1)S(1)} async-done(((bf16[8,256,256]{2,1,0:T(8,128)(2,1)}), bf16[8,256,256]{2,1,0:T(8,128)(2,1)S(1)}, u32[]{:S(2)}, u32[]{:S(2)}) %all-to-all-start.1) | async-done | bytes 1048608 | tf_op jit(solution)/shard_map/all_to_all | solution.py:613
  53.3 0.0 copy-start.18
  53.3 1.0 copy-done.18
  54.3 0.0 copy-start.6
  54.3 0.0 copy-start.7
  54.3 0.0 copy-start.16
  54.3 0.0 copy-start.17
  54.3 16.6 %shard_map.166 = (bf16[8,64,512]{2,1,0:T(8,128)(2,1)}, bf16[8,64,512]{2,1,0:T(8,128)(2,1)}, f32[64,512]{1,0:T(8,128)}, bf16[256,256]{1,0:T(8,128)(2,1)}, bf16[64,10240]{1,0:T(8,128)(2,1)}) custom-call(s32[1,128]{1,0:T(1,128)} %get-tuple-element.36.refs_0_, s32[1]{0:T(128)} %bitcast.core_ref.refs_0_.refs_1_, bf16[8,256,256]{2,1,0:T(8,128)(2,1)} %copy-done.18, ...), custom_call_target="tpu_custom_call" | custom-call | tf_op jit(solution)/shard_map/pallas_call | solution.py:85
  70.8 0.0 copy-done.6
  70.9 0.0 copy-done.7
  70.9 0.0 copy-done.16
  70.9 0.0 copy-done.17
  70.9 0.0 copy-start.8
  70.9 1.3 copy-done.8
  72.2 0.0 copy-start.15
  72.2 0.9 copy-done.15
  73.1 0.0 copy-start.10
  73.1 0.0 copy-start.11
  73.1 6.2 %shard_map.167 = (bf16[8,256,256]{2,1,0:T(8,128)(2,1)S(1)}, f32[16,64]{1,0:T(8,128)S(1)}) custom-call(s32[1,128]{1,0:T(1,128)S(1)} %copy-done.17, bf16[256,256]{1,0:T(8,128)(2,1)S(1)} %copy-done.15, s32[8,10240]{1,0:T(8,128)S(1)} %copy-done.6, bf16[16,10240]{1,0:T(8,128)(2,1)S(1)} %copy-done.7, bf16[64,16]{1,0:T(8,128)(2,1)S(1)} %copy-done.16, ...), custom_call_target="tpu_custom_call" | custom-call | tf_op jit(solution)/shard_map/pallas_call | solution.py:85
  79.4 0.0 copy-start.1
  79.4 0.0 copy-start.4
  79.4 0.0 copy-start.14
  79.4 20.0 %all_to_all.26.refs_1_ = bf16[8,256,256]{2,1,0:T(8,128)(2,1)S(1)} all-to-all(bf16[8,256,256]{2,1,0:T(8,128)(2,1)S(1)} %get-tuple-element.47), channel_id=1, replica_groups=mesh['dp'=16,'graph'=8] {'graph'}, dimensions={0} | all-to-all | bytes 2097152 | tf_op jit(solution)/shard_map/all_to_all | solution.py:638
  99.4 0.0 copy-done.10
  99.4 0.0 copy-done.11
  99.4 0.0 copy-done.1
  99.4 0.0 copy-done.4
  99.4 0.0 copy-done.14
  99.4 0.0 copy-start.12
  99.5 1.0 copy-done.12
  100.5 0.0 copy-start.13
  100.5 1.0 copy-done.13
  101.5 2.0 %shard_map.168 = (bf16[1024,512]{1,0:T(8,128)(2,1)S(1)}, bf16[8,112,512]{2,1,0:T(8,128)(2,1)S(1)}, bf16[8,112,512]{2,1,0:T(8,128)(2,1)S(1)}) custom-call(s32[1]{0:T(128)} %bitcast.core_ref.refs_0_.refs_1_, bf16[8,256,256]{2,1,0:T(8,128)(2,1)S(1)} %all_to_all.26.refs_1_, bf16[1024,512]{1,0:T(8,128)(2,1)S(1)} %copy-done.10, bf16[1024,512]{1,0:T(8,128)(2,1)S(1)} %copy-done.11, ...), custom_call_target="tpu_custom_call" | custom-call | tf_op jit(solution)/shard_map/pallas_call | solution.py:85
  103.6 0.1 collective-permute-start.1
  103.6 1.7 %shard_map.169 = bf16[1024,512]{1,0:T(8,128)(2,1)} custom-call(bf16[1024,512]{1,0:T(8,128)(2,1)S(1)} %get-tuple-element.55.dz_ref, bf16[512,640]{1,0:T(8,128)(2,1)S(1)} %copy-done.4), custom_call_target="tpu_custom_call" | custom-call | tf_op jit(solution)/shard_map/pallas_call | solution.py:85
  105.4 0.8 collective-permute-done.1.other_ref
  106.1 0.2 shard_map.170
  106.3 17.4 %all_to_all.27.parts_ref = bf16[8,112,512]{2,1,0:T(8,128)(2,1)S(1)} all-to-all(bf16[8,112,512]{2,1,0:T(8,128)(2,1)S(1)} %shard_map.170), channel_id=1, replica_groups={{0,16,32,48,64,80,96,112},{8,24,40,56,72,88,104,120},{1,17,33,49,65,81,..., dimensions={0} | all-to-all | bytes 1835008 | tf_op jit(solution)/shard_map/all_to_all | solution.py:666
  123.7 0.1 shard_map.171
  123.8 18.0 %all_to_all.28.parts_ref = bf16[8,112,512]{2,1,0:T(8,128)(2,1)S(1)} all-to-all(bf16[8,112,512]{2,1,0:T(8,128)(2,1)S(1)} %shard_map.171), channel_id=1, replica_groups=mesh['dp'=16,'graph'=8] {'graph'}, dimensions={0} | all-to-all | bytes 1835008 | tf_op jit(solution)/shard_map/all_to_all | solution.py:673
  141.8 0.7 shard_map.172
Async XLA Ops:
  0.6 25.2 %copy-start = (bf16[1024,512]{1,0:T(8,128)(2,1)S(1)}, bf16[1024,512]{1,0:T(8,128)(2,1)}, u32[]{:S(2)}) copy-start(bf16[1024,512]{1,0:T(8,128)(2,1)} %refs_4_.3) | copy-start | bytes 3145732
  23.4 3.9 %copy-start.2 = (bf16[8,112,512]{2,1,0:T(8,128)(2,1)}, bf16[8,112,512]{2,1,0:T(8,128)(2,1)S(1)}, u32[]{:S(2)}) copy-start(bf16[8,112,512]{2,1,0:T(8,128)(2,1)S(1)} %all_to_all.25.own_ref.refs_3_) | copy-start | bytes 2752516
  23.4 2.5 %collective-permute-start = (bf16[8,112,512]{2,1,0:T(8,128)(2,1)S(1)}, bf16[8,112,512]{2,1,0:T(8,128)(2,1)S(1)}, u32[]{:S(2)}, u32[]{:S(2)}) collective-permute-start(bf16[8,112,512]{2,1,0:T(8,128)(2,1)S(1)} %all_to_all.25.own_ref.refs_3_), channel_id=1, source_target_pairs={{0,8},{8,0},{16,24},{24,16},{32,40},{40,32},{48,56},{56,48},{64,72... | collective-permute-start | bytes 2752520 | tf_op jit(solution)/shard_map/ppermute | solution.py:581
  25.8 1.5 %copy-start.5 = (bf16[8,112,512]{2,1,0:T(8,128)(2,1)}, bf16[8,112,512]{2,1,0:T(8,128)(2,1)S(1)}, u32[]{:S(2)}) copy-start(bf16[8,112,512]{2,1,0:T(8,128)(2,1)S(1)} %collective-permute-done.other_ref.refs_4_) | copy-start | bytes 2752516
  27.3 0.8 copy-start.3
  28.1 1.0 copy-start.9
  29.1 24.2 %all-to-all-start.1 = ((bf16[8,256,256]{2,1,0:T(8,128)(2,1)}), bf16[8,256,256]{2,1,0:T(8,128)(2,1)S(1)}, u32[]{:S(2)}, u32[]{:S(2)}) async-start(bf16[8,256,256]{2,1,0:T(8,128)(2,1)} %copy-done.9), calls=%async_computation.1 | async-start | bytes 2097152 | tf_op jit(solution)/shard_map/all_to_all | solution.py:613
  53.3 1.0 copy-start.18
  54.3 16.6 %copy-start.6 = (s32[8,10240]{1,0:T(8,128)S(1)}, s32[8,10240]{1,0:T(8,128)}, u32[]{:S(2)}) copy-start(s32[8,10240]{1,0:T(8,128)} %get-tuple-element.38.refs_3_.refs_2_) | copy-start | bytes 983044
  54.3 16.6 %copy-start.7 = (bf16[16,10240]{1,0:T(8,128)(2,1)S(1)}, bf16[16,10240]{1,0:T(8,128)(2,1)}, u32[]{:S(2)}) copy-start(bf16[16,10240]{1,0:T(8,128)(2,1)} %get-tuple-element.39.refs_4_.refs_3_) | copy-start | bytes 983044
  54.3 16.6 %copy-start.16 = (bf16[64,16]{1,0:T(8,128)(2,1)S(1)}, bf16[64,16]{1,0:T(8,128)(2,1)}, u32[]{:S(2)}) copy-start(bf16[64,16]{1,0:T(8,128)(2,1)} %get-tuple-element.41.refs_5_.refs_4_) | copy-start | bytes 6148
  54.3 16.6 %copy-start.17 = (s32[1,128]{1,0:T(1,128)S(1)}, s32[1,128]{1,0:T(1,128)}, u32[]{:S(2)}) copy-start(s32[1,128]{1,0:T(1,128)} %get-tuple-element.36.refs_0_) | copy-start | bytes 1540
  70.9 1.3 copy-start.8
  72.2 0.9 copy-start.15
  73.1 26.3 %copy-start.10 = (bf16[1024,512]{1,0:T(8,128)(2,1)S(1)}, bf16[1024,512]{1,0:T(8,128)(2,1)}, u32[]{:S(2)}) copy-start(bf16[1024,512]{1,0:T(8,128)(2,1)} %get-tuple-element.48.refs_2_) | copy-start | bytes 3145732
  73.1 26.3 %copy-start.11 = (bf16[1024,512]{1,0:T(8,128)(2,1)S(1)}, bf16[1024,512]{1,0:T(8,128)(2,1)}, u32[]{:S(2)}) copy-start(bf16[1024,512]{1,0:T(8,128)(2,1)} %get-tuple-element.49.refs_3_) | copy-start | bytes 3145732
  79.4 20.1 %copy-start.1 = (bf16[1024,512]{1,0:T(8,128)(2,1)S(1)}, bf16[1024,512]{1,0:T(8,128)(2,1)}, u32[]{:S(2)}) copy-start(bf16[1024,512]{1,0:T(8,128)(2,1)} %refs_4_.3) | copy-start | bytes 3145732
  79.4 20.1 %copy-start.4 = (bf16[512,640]{1,0:T(8,128)(2,1)S(1)}, bf16[512,640]{1,0:T(8,128)(2,1)}, u32[]{:S(2)}) copy-start(bf16[512,640]{1,0:T(8,128)(2,1)} %copy-done.3) | copy-start | bytes 1966084
  79.4 20.1 %copy-start.14 = (f32[64,512]{1,0:T(8,128)S(1)}, f32[64,512]{1,0:T(8,128)}, u32[]{:S(2)}) copy-start(f32[64,512]{1,0:T(8,128)} %get-tuple-element.51.refs_7_) | copy-start | bytes 393220
  99.4 1.0 copy-start.12
  100.5 1.0 copy-start.13
  103.6 2.6 %collective-permute-start.1 = (bf16[8,112,512]{2,1,0:T(8,128)(2,1)S(1)}, bf16[8,112,512]{2,1,0:T(8,128)(2,1)S(1)}, u32[]{:S(2)}, u32[]{:S(2)}) collective-permute-start(bf16[8,112,512]{2,1,0:T(8,128)(2,1)S(1)} %get-tuple-element.54), channel_id=1, source_target_pairs={{0,8},{8,0},{16,24},{24,16},{32,40},{40,32},{48,56},{56,48},{64,72... | collective-permute-start | bytes 2752520 | tf_op jit(solution)/shard_map/ppermute | solution.py:581

commit v2 on v1

--- a/solution.py
+++ b/solution.py
@@ -161,25 +161,29 @@
         rows_ref[:, cols] = acc[base + nb : base + nb + extra, :].astype(jnp.int32)
 
 
-def forward_kernel(
+def rows_of(owner, share):
+    return pl.ds(pl.multiple_of(owner * share, share), share)
+
+
+def middle_kernel(
     ready,
-    owner_ref,
+    slot_ref,
     core_ref,
     down_ref,
     rows_ref,
     basis_ref,
-    w_basis_ref,
-    w_up_ref,
-    w_first_ref,
-    w_second_ref,
+    own_ref,
+    other_ref,
     cot_ref,
+    partial_ref,
     early_ref,
     early_other_ref,
     up_grad_ref,
-    dagg_ref,
-    down_in_ref,
-    second_s,
-    first_s,
+    basis_grad_ref,
+    w_first_s,
+    w_second_s,
+    up_s,
+    basis_s,
     agg_acc,
     agg_s,
     mixed_s,
@@ -187,12 +191,32 @@
     dz_four_s,
     dz_three_s,
     dz_two_s,
+    dagg_s,
+    down_in_s,
+    coeff_s,
+    total,
 ):
     peers, stack_rows, e_hi = down_ref.shape
     slots = rows_ref.shape[1]
-    trip = w_up_ref.shape[0]
-    parts = stack_rows // trip
+    pairs = own_ref.shape[0]
+    parts = mixed_s.shape[0] // e_hi
+    trip = stack_rows // parts
     width = GROUP * CHUNK
+    share = w_first_s.shape[0] // (2 * pairs)
+    up_rows = up_s.shape[1]
+    core = core_ref[0]
+
+    for pair in range(pairs):
+        for ref, side in ((own_ref, core), (other_ref, 1 - core)):
+            owner = 2 * pair + side
+            w_second_s[rows_of(owner, share), :] = ref[pair, share : 2 * share, :]
+            w_first_s[rows_of(owner, share), :] = ref[pair, 2 * share : 3 * share, :]
+            small = ref[pair, 3 * share :, :].astype(F32)
+            up_s[owner] = small[:up_rows]
+            basis_s[owner] = small[up_rows : up_rows + 1, :LANES]
+    w_up = jnp.concatenate([up_s[k] for k in range(2 * pairs)], axis=0).astype(BF16)
+    w_basis = jnp.concatenate([basis_s[k] for k in range(2 * pairs)], axis=0)
+    w_basis = w_basis.T[:trip].astype(BF16)
     agg_acc[...] = jnp.zeros_like(agg_acc)
 
     def forward(step, carry):
@@ -200,12 +224,13 @@
         found = []
         for k in range(GROUP):
             here = pl.ds(pl.multiple_of(step * width + k * CHUNK, CHUNK), CHUNK)
-            owner = owner_ref[0, step * GROUP + k]
+            slot = slot_ref[0, step * GROUP + k]
             hot = one_hot(rows_ref[0:1, here], e_hi)
-            found.append(pick(dot(down_ref[owner], hot), rows_ref[1:2, here], parts))
+            found.append(pick(dot(down_ref[slot], hot), rows_ref[1:2, here], parts))
         down_in = jnp.concatenate(found, axis=1)
-        coeff = dot(w_basis_ref[...], basis_ref[:, cols])
-        down_in_ref[:, cols] = down_in.astype(BF16)
+        coeff = dot(w_basis, basis_ref[:, cols])
+        down_in_s[:, cols] = down_in.astype(BF16)
+        coeff_s[:, cols] = coeff
         hot_e = one_hot(rows_ref[2:3, cols], e_hi)
         placed = spread(down_in * coeff, rows_ref[3:4, cols], parts)
         agg_acc[...] += dot(hot_e, placed, NT)
@@ -214,14 +239,15 @@
     lax.fori_loop(0, slots // width, forward, 0)
 
     ready()
-    w_up = w_up_ref[...]
-    w_first = w_first_ref[...]
-    w_second = w_second_ref[...]
+    w_first = w_first_s[...]
+    w_second = w_second_s[...]
     for q in range(parts):
         rows = slice(q * e_hi, (q + 1) * e_hi)
-        agg = agg_acc[:, q * trip : (q + 1) * trip].astype(BF16)
-        agg_s[rows, :] = agg
-        act, slope_two = silu_and_slope(dot(agg, w_up))
+        agg_s[rows, :] = agg_acc[:, q * trip : (q + 1) * trip].astype(BF16)
+    step = 2 * e_hi
+    for start in range(0, mixed_s.shape[0], step):
+        rows = slice(start, start + step)
+        act, slope_two = silu_and_slope(dot(agg_s[rows, :], w_up))
         mixed = act.astype(BF16)
         mixed_s[rows, :] = mixed
         act, slope_three = silu_and_slope(dot(mixed, w_first))
@@ -233,49 +259,37 @@
         dz_four_s[rows, :] = dz_four
         dz_three = (dot(dz_four, w_second, NT) * slope_three).astype(BF16)
         dz_three_s[rows, :] = dz_three
-        dz_two = ((cot + dot(dz_three, w_first, NT)) * slope_two).astype(BF16)
-        dz_two_s[rows, :] = dz_two
-        dagg_ref[q * trip : (q + 1) * trip, :] = dot(w_up, dz_two, NT).astype(BF16)
-
-    second_s[...] = dot(inner_s[...], dz_four_s[...], TN).astype(BF16)
-    first_s[...] = dot(mixed_s[...], dz_three_s[...], TN).astype(BF16)
+        dz_two_s[rows, :] = ((cot + dot(dz_three, w_first, NT)) * slope_two).astype(BF16)
+    for q in range(parts):
+        rows = slice(q * e_hi, (q + 1) * e_hi)
+        dagg_s[q * trip : (q + 1) * trip, :] = dot(w_up, dz_two_s[rows, :], NT).astype(BF16)
+
+    w_second_s[...] = dot(inner_s[...], dz_four_s[...], TN).astype(BF16)
+    w_first_s[...] = dot(mixed_s[...], dz_three_s[...], TN).astype(BF16)
     up_grad_ref[...] = dot(agg_s[...], dz_two_s[...], TN)
-    pairs = early_ref.shape[0]
-    share = w_first.shape[0] // (2 * pairs)
-    core = core_ref[0]
     for pair in range(pairs):
         for ref, side in ((early_ref, core), (early_other_ref, 1 - core)):
-            at = pl.ds(pl.multiple_of((2 * pair + side) * share, share), share)
-            ref[pair, :share, :] = second_s[at, :]
-            ref[pair, share:, :] = first_s[at, :]
-
-
-def backward_kernel(
-    owner_ref, dagg_ref, rows_ref, basis_ref, w_basis_ref, down_in_ref, partial_ref, basis_grad, total
-):
-    peers, stack_rows, e_hi = partial_ref.shape
-    slots = rows_ref.shape[1]
-    trip = w_basis_ref.shape[0]
-    parts = stack_rows // trip
-    width = GROUP * CHUNK
-    basis_grad[...] = jnp.zeros_like(basis_grad)
+            at = rows_of(2 * pair + side, share)
+            ref[pair, :share, :] = w_second_s[at, :]
+            ref[pair, share:, :] = w_first_s[at, :]
+
+    basis_grad_ref[...] = jnp.zeros_like(basis_grad_ref)
     total[...] = jnp.zeros_like(total)
 
     def backward(step, carry):
         cols = pl.ds(pl.multiple_of(step * width, width), width)
         hot_e = one_hot(rows_ref[2:3, cols], e_hi)
-        dagg_out = pick(dot(dagg_ref[...], hot_e), rows_ref[3:4, cols], parts)
-        dcoeff = (dagg_out * down_in_ref[:, cols].astype(F32)).astype(BF16)
-        basis_grad[...] += dot(basis_ref[:, cols], dcoeff, NT)
-        coeff = dot(w_basis_ref[...], basis_ref[:, cols])
-        placed = spread(dagg_out * coeff, rows_ref[1:2, cols], parts)
+        dagg_out = pick(dot(dagg_s[...], hot_e), rows_ref[3:4, cols], parts)
+        dcoeff = (dagg_out * down_in_s[:, cols].astype(F32)).astype(BF16)
+        basis_grad_ref[...] += dot(basis_ref[:, cols], dcoeff, NT)
+        placed = spread(dagg_out * coeff_s[:, cols], rows_ref[1:2, cols], parts)
         hot = one_hot(rows_ref[0:1, cols], e_hi)
         terms = []
         for k in range(GROUP):
             here = slice(k * CHUNK, (k + 1) * CHUNK)
             terms.append(dot(placed[:, here], hot[:, here], NT))
         for k in range(GROUP):
-            total[owner_ref[0, step * GROUP + k]] += terms[k]
+            total[slot_ref[0, step * GROUP + k]] += terms[k]
         return carry
 
     lax.fori_loop(0, slots // width, backward, 0)
@@ -303,64 +317,45 @@
     )
 
 
-def forward(owner, core, down, rows, basis, w_basis_t, w_up, w_first, w_second, cot):
+def middle(slot, core, down, rows, basis, own, other, cot):
     shape = jax.ShapeDtypeStruct
     vmem = pltpu.VMEM
     edges, width = cot.shape
-    trip = w_up.shape[0]
+    peers, stack_rows, e_hi = down.shape
+    trip = stack_rows * e_hi // edges
     nb = basis.shape[0]
     slots = rows.shape[1]
+    half = shape((nb // 2, 2 * width // nb, width), BF16)
     return call(
-        forward_kernel,
-        (
-            shape((nb // 2, 2 * width // nb, width), BF16),
-            shape((nb // 2, 2 * width // nb, width), BF16),
-            shape((trip, width), F32),
-            shape((edges // CHUNK * trip, CHUNK), BF16),
-            shape((trip, slots), BF16),
-        ),
-        owner,
+        middle_kernel,
+        (shape(down.shape, BF16), half, half, shape((trip, width), F32), shape((nb, trip), F32)),
+        slot,
         core,
         down,
         rows,
         basis,
-        w_basis_t,
-        w_up,
-        w_first,
-        w_second,
+        own,
+        other,
         cot,
         scratch=[
             vmem((width, width), BF16),
             vmem((width, width), BF16),
-            vmem((CHUNK, edges // CHUNK * trip), F32),
+            vmem((nb, trip // nb, width), F32),
+            vmem((nb, 1, LANES), F32),
+            vmem((e_hi, stack_rows), F32),
             vmem((edges, trip), BF16),
         ]
-        + [vmem((edges, width), BF16)] * 5,
+        + [vmem((edges, width), BF16)] * 5
+        + [
+            vmem((stack_rows, e_hi), BF16),
+            vmem((trip, slots), BF16),
+            vmem((trip, slots), F32),
+            vmem(down.shape, F32),
+        ],
         smem=(0, 1),
-        hbm=(2, 3, 4, 5),
-        lazy=(6, 7, 8, 9),
+        hbm=(2, 3, 4, 5, 6),
+        lazy=(7,),
         vmem=60,
-    )
-
-
-def backward(owner, dagg, rows, basis, w_basis_t, down_in, peers):
-    shape = jax.ShapeDtypeStruct
-    nb = basis.shape[0]
-    trip = w_basis_t.shape[0]
-    stack = (peers,) + dagg.shape
-    return call(
-        backward_kernel,
-        (shape(stack, BF16), shape((nb, trip), F32)),
-        owner,
-        dagg,
-        rows,
-        basis,
-        w_basis_t,
-        down_in,
-        scratch=[pltpu.VMEM(stack, F32)],
-        smem=(0,),
-        hbm=(2, 3),
-        vmem=40,
     )
 
 
@@ -417,51 +412,9 @@
             down_ref[peer, part * trip : (part + 1) * trip, :] = down_t
 
 
-def hidden_kernel(
-    core_ref,
-    feats_ref,
-    weights_ref,
-    own_ref,
-    other_ref,
-    hidden_ref,
-    slope_ref,
-    second_ref,
-    first_ref,
-    up_ref,
-    basis_ref,
-    up_s,
-    basis_s,
-):
-    rows, width = feats_ref.shape
-    pairs = own_ref.shape[0]
-    share = width // (2 * pairs)
-    up_rows = up_ref.shape[0] // (2 * pairs)
-    trip = basis_ref.shape[0]
-    core = core_ref[0]
-    for pair in range(pairs):
-        for ref, side in ((own_ref, core), (other_ref, 1 - core)):
-            at = pl.ds(pl.multiple_of((2 * pair + side) * share, share), share)
-            second_ref[at, :] = ref[pair, share : 2 * share, :]
-            first_ref[at, :] = ref[pair, 2 * share : 3 * share, :]
-            small = ref[pair, 3 * share :, :].astype(F32)
-            up_s[2 * pair + side] = small[:up_rows]
-            basis_s[2 * pair + side] = small[up_rows : up_rows + 1, :LANES]
-    up_ref[...] = jnp.concatenate([up_s[k] for k in range(2 * pairs)], axis=0).astype(BF16)
-    basis = jnp.concatenate([basis_s[k] for k in range(2 * pairs)], axis=0)
-    basis_ref[...] = basis.T[:trip].astype(BF16)
-    w_pair = weights_ref[:, :width]
-    for first in range(0, rows, CHUNK):
-        block = slice(first, first + CHUNK)
-        act, slope = silu_and_slope(dot(feats_ref[block, :], w_pair))
-        hidden_ref[block, :] = act.astype(BF16)
-        slope_ref[block, :] = slope.astype(BF16)
-
-
 def tail_kernel(
     core_ref,
     parts_ref,
-    hidden_ref,
-    slope_ref,
     feats_ref,
     weights_ref,
     basis_ref,
@@ -471,6 +424,7 @@
     dz_ref,
     mine_ref,
     theirs_ref,
+    hidden_s,
     ddown_s,
     pair_s,
     small,
@@ -487,12 +441,13 @@
             part * trip : (part + 1) * trip, :
         ].T.astype(BF16)
     w_down = weights_ref[:, width : width + trip]
-    for first in range(0, rows, 256):
-        block = slice(first, first + 256)
-        dz_ref[block, :] = (
-            dot(ddown_s[block, :], w_down, NT) * slope_ref[block, :].astype(F32)
-        ).astype(BF16)
-    down = dot(hidden_ref[...], ddown_s[...], TN)
+    w_pair = weights_ref[:, :width]
+    for first in range(0, rows, 512):
+        block = slice(first, first + 512)
+        act, slope = silu_and_slope(dot(feats_ref[block, :], w_pair))
+        hidden_s[block, :] = act.astype(BF16)
+        dz_ref[block, :] = (dot(ddown_s[block, :], w_down, NT) * slope).astype(BF16)
+    down = dot(hidden_s[...], ddown_s[...], TN)
     pair_s[...] = dot(feats_ref[...], dz_ref[...], TN).astype(BF16)
     owners = basis_ref.shape[0]
     share = width // owners
@@ -509,8 +464,7 @@
             (theirs_ref, 1 - core, early_other_ref),
         ):
             owner = 2 * pair + side
-            at = pl.ds(pl.multiple_of(owner * share, share), share)
-            ref[pair, :share, :] = pair_s[at, :]
+            ref[pair, :share, :] = pair_s[rows_of(owner, share), :]
             ref[pair, share : share + SMALL_ROWS, :] = small[owner].astype(BF16)
             ref[pair, share + SMALL_ROWS :, :] = half[pair]
 
@@ -594,9 +548,11 @@
         hbm=range(6),
         vmem=60,
     )
+    own, source_edge = lax.optimization_barrier((own, source_edge))
     own = lax.all_to_all(own, "dp", 0, 0, axis_index_groups=same_core)
+    index, basis, slot = order(source_edge, target_edge, angle_basis, peers, rows)
+    own, index = lax.optimization_barrier((own, index))
     other = swap(own)
-    index, basis, owner = order(source_edge, target_edge, angle_basis, peers, rows)
     down, head = call(
         down_kernel,
         (
@@ -611,30 +567,9 @@
         vmem=16,
     )
     down = lax.all_to_all(down, "graph", 0, 0)
-    hidden, slope, w_second, w_first, w_up, w_basis_t = call(
-        hidden_kernel,
-        (
-            shape((rows, width), BF16),
-            shape((rows, width), BF16),
-            shape((width, width), BF16),
-            shape((width, width), BF16),
-            shape((trip, width), BF16),
-            shape((trip, nb), BF16),
-        ),
-        core,
-        edge_feats,
-        head,
-        own,
-        other,
-        scratch=[vmem((owners, up_rows, width), F32), vmem((owners, 1, LANES), F32)],
-        smem=(0,),
-        hbm=(1, 2, 3, 4),
-        vmem=60,
-    )
-    early, early_other, up_grad, dagg, down_in = forward(
-        owner, core, down, index, basis, w_basis_t, w_up, w_first, w_second, cotangent
-    )
-    partial, basis_grad = backward(owner, dagg, index, basis, w_basis_t, down_in, peers)
+    partial, early, early_other, up_grad, basis_grad = middle(
+        slot, core, down, index, basis, own, other, cotangent
+    )
     parts = lax.all_to_all(partial, "graph", 0, 0)
     half = shape((pairs, 3 * share + SMALL_ROWS, width), BF16)
     dz_one, grads, other = call(
@@ -642,8 +577,6 @@
         (shape((rows, width), BF16), half, half),
         core,
         parts,
-        hidden,
-        slope,
         edge_feats,
         head,
         basis_grad,
@@ -651,12 +584,12 @@
         early,
         early_other,
         scratch=[
+            vmem((rows, width), BF16),
             vmem((rows, trip), BF16),
             vmem((width, width), BF16),
             vmem((owners, SMALL_ROWS, width), F32),
         ],
         smem=(0,),
-        hbm=(2, 3, 4, 5, 8, 9),
         vmem=32,
     )
     other = swap(other)

time: 143 us -> 134 us (0.937)
  Pallas kernels: 43.5 us -> 36.6 us
  local copies, waits for them, and re-layouts: 7.11 us -> 0.71 us
  blocking collectives: 76.1 us -> 79.3 us
    pallas_call x11 -> x9, Pallas kernels: 43.5 us -> 36.6 us  [call(): pl.pallas_call(body if fetched else kernel, out_shape=out_shape, in_specs...]
    unnamed x38 -> x14, local copies, waits for them, and re-layouts: 7.11 us -> 0.71 us
    all_to_all x1, blocking collectives: 20.7 us -> 24 us  [on_device(): down = lax.all_to_all(down, 'graph', 0, 0)]
  transfers between devices with their start and end apart: 3 -> 3, of which waited for: 3 -> 3; matrix products, arithmetic and copies ran while one was open for 0% -> 0% of each run, Pallas kernels for 10% -> 7%
where the time goes in v2:
time: 134 us; the launch traced here: 133 us
  blocking collectives  79.3 us (59%)
  Pallas kernels  36.6 us (27%)
  waiting for transfers between devices  9.53 us (7%)
  starting transfers between devices  6.56 us (5%)
    pallas_call x9, Pallas kernels, call(): pl.pallas_call(body if fetched else kernel, out_shape=out_shape, in_specs...  36.6 us
    all_to_all x1, blocking collectives, on_device(): down = lax.all_to_all(down, 'graph', 0, 0)  24 us
    all_to_all x1, blocking collectives, on_device(): parts = lax.all_to_all(partial, 'graph', 0, 0)  19.9 us
    all_to_all x1, blocking collectives, on_device(): sums = lax.all_to_all(sums, 'graph', 0, 0)  18 us
    all_to_all x1, blocking collectives, on_device(): chip = lax.all_to_all(chip, 'dp', 0, 0, axis_index_groups=same_core)  17.4 us
    all_to_all x1, starting transfers between devices, on_device(): own = lax.all_to_all(own, 'dp', 0, 0, axis_index_groups=same_core)  6.47 us
    all_to_all x1, waiting for transfers between devices, on_device(): own = lax.all_to_all(own, 'dp', 0, 0, axis_index_groups=same_core)  6.31 us
    ppermute x2, waiting for transfers between devices, swap(): lax.ppermute(value, 'dp', [(owner, owner ^ 1) for owner in range(owners)])  3.21 us
  transfers between devices with their start and end apart: 3, of which 3 were waited for; matrix products, arithmetic and copies ran while one was open for 0% of the time, Pallas kernels for 7%

profile of v2, /device:TPU:0, one launch (start us, length us, event | category | flops | bytes accessed | tf_op | source)
XLA Modules:
  0.0 133.5 jit_solution(14892674259916889628)
XLA Ops:
  0.6 1.9 %shard_map.162 = bf16[8,112,512]{2,1,0:T(8,128)(2,1)} custom-call(bf16[32,512]{1,0:T(8,128)(2,1)} %refs_0_.1, bf16[32,64]{1,0:T(8,128)(2,1)} %refs_1_.1, bf16[1,64]{1,0:T(2,128)(2,1)} %refs_2_.2, bf16[4,512]{1,0:T(4,128)(2,1)} %refs_3_.1, bf16[32,512]{1,0:T(8,128)(2,1)} %refs_4_.1, bf16[32,512]{1,0:T(8,128)(2,1)} %refs_5_.1), custom_call_target="tpu_custom_call" | custom-call | tf_op jit(solution)/shard_map/pallas_call | solution.py:85
  2.5 0.0 copy-start.1
  2.5 6.5 %all-to-all-start = ((bf16[8,112,512]{2,1,0:T(8,128)(2,1)}), bf16[8,112,512]{2,1,0:T(8,128)(2,1)S(1)}, u32[]{:S(2)}, u32[]{:S(2)}) async-start(bf16[8,112,512]{2,1,0:T(8,128)(2,1)} %shard_map.162), calls=%async_computation | async-start | bytes 1835008 | tf_op jit(solution)/shard_map/all_to_all | solution.py:552
  9.0 8.0 %shard_map.163 = (s32[8,10240]{1,0:T(8,128)}, bf16[16,10240]{1,0:T(8,128)(2,1)}, s32[1,128]{1,0:T(1,128)}) custom-call(s32[64,128]{1,0:T(8,128)} %bitcast.3, s32[64,128]{1,0:T(8,128)} %bitcast.4, bf16[16,8192]{1,0:T(8,128)(2,1)} %refs_2_.3), custom_call_target="tpu_custom_call" | custom-call | tf_op jit(solution)/shard_map/pallas_call | solution.py:85
  17.0 6.3 %all-to-all-done.own_ref.refs_5_ = bf16[8,112,512]{2,1,0:T(8,128)(2,1)S(1)} async-done(((bf16[8,112,512]{2,1,0:T(8,128)(2,1)}), bf16[8,112,512]{2,1,0:T(8,128)(2,1)S(1)}, u32[]{:S(2)}, u32[]{:S(2)}) %all-to-all-start) | async-done | bytes 917536 | tf_op jit(solution)/shard_map/all_to_all | solution.py:552
  23.3 0.0 copy-start
  23.3 0.0 collective-permute-start
  23.3 2.5 %collective-permute-done.other_ref.refs_6_ = bf16[8,112,512]{2,1,0:T(8,128)(2,1)S(1)} collective-permute-done((bf16[8,112,512]{2,1,0:T(8,128)(2,1)S(1)}, bf16[8,112,512]{2,1,0:T(8,128)(2,1)S(1)}, u32[]{:S(2)}, u32[]{:S(2)}) %collective-permute-start) | collective-permute-done | bytes 917536 | tf_op jit(solution)/shard_map/ppermute | solution.py:535
  25.8 0.0 copy-start.2
  25.8 0.0 copy-done.1
  25.8 1.4 %shard_map.164 = (bf16[8,256,256]{2,1,0:T(8,128)(2,1)S(1)}, bf16[512,640]{1,0:T(8,128)(2,1)S(1)}) custom-call(s32[1]{0:T(128)} %bitcast.core_ref.refs_1_, bf16[1024,512]{1,0:T(8,128)(2,1)S(1)} %copy-done.1, bf16[8,112,512]{2,1,0:T(8,128)(2,1)S(1)} %all-to-all-done.own_ref.refs_5_, bf16[8,112,512]{2,1,0:T(8,128)(2,1)S(1)} %collective-permute-done.other_ref.refs_6_), custom_call_target="tpu_custom_call" | custom-call | tf_op jit(solution)/shard_map/pallas_call | solution.py:85
  27.2 0.0 copy-done
  27.2 0.0 copy-done.2
  27.2 24.0 %all_to_all.25.refs_2_ = bf16[8,256,256]{2,1,0:T(8,128)(2,1)} all-to-all(bf16[8,256,256]{2,1,0:T(8,128)(2,1)S(1)} %get-tuple-element.37), channel_id=1, replica_groups=mesh['dp'=16,'graph'=8] {'graph'}, dimensions={0} | all-to-all | bytes 2097152 | tf_op jit(solution)/shard_map/all_to_all | solution.py:569
  51.3 20.4 %shard_map.165 = (bf16[8,256,256]{2,1,0:T(8,128)(2,1)}, bf16[8,64,512]{2,1,0:T(8,128)(2,1)}, bf16[8,64,512]{2,1,0:T(8,128)(2,1)}, f32[64,512]{1,0:T(8,128)}, f32[16,64]{1,0:T(8,128)}) custom-call(s32[1,128]{1,0:T(1,128)} %get-tuple-element.33.refs_0_, s32[1]{0:T(128)} %bitcast.core_ref.refs_1_, bf16[8,256,256]{2,1,0:T(8,128)(2,1)} %all_to_all.25.refs_2_, ...), custom_call_target="tpu_custom_call" | custom-call | tf_op jit(solution)/shard_map/pallas_call | solution.py:85
  71.7 0.0 copy-start.3
  71.7 0.0 copy-start.4
  71.7 0.0 copy-start.5
  71.7 19.9 %all_to_all.26.parts_ref = bf16[8,256,256]{2,1,0:T(8,128)(2,1)S(1)} all-to-all(bf16[8,256,256]{2,1,0:T(8,128)(2,1)} %get-tuple-element.40), channel_id=1, replica_groups=mesh['dp'=16,'graph'=8] {'graph'}, dimensions={0} | all-to-all | bytes 2097152 | tf_op jit(solution)/shard_map/all_to_all | solution.py:573
  91.6 0.0 copy-start.6
  91.6 0.0 copy-done.3
  91.6 0.0 copy-done.4
  91.6 0.0 copy-done.5
  91.7 0.7 copy-done.6
  92.3 2.1 %shard_map.166 = (bf16[1024,512]{1,0:T(8,128)(2,1)S(1)}, bf16[8,112,512]{2,1,0:T(8,128)(2,1)S(1)}, bf16[8,112,512]{2,1,0:T(8,128)(2,1)S(1)}) custom-call(s32[1]{0:T(128)} %bitcast.core_ref.refs_1_, bf16[8,256,256]{2,1,0:T(8,128)(2,1)S(1)} %all_to_all.26.parts_ref, bf16[1024,512]{1,0:T(8,128)(2,1)S(1)} %copy-done.1, ...), custom_call_target="tpu_custom_call" | custom-call | tf_op jit(solution)/shard_map/pallas_call | solution.py:85
  94.5 0.1 collective-permute-start.1
  94.6 1.7 %shard_map.167 = bf16[1024,512]{1,0:T(8,128)(2,1)} custom-call(bf16[1024,512]{1,0:T(8,128)(2,1)S(1)} %get-tuple-element.47.dz_ref, bf16[512,640]{1,0:T(8,128)(2,1)S(1)} %get-tuple-element.41.weights_ref), custom_call_target="tpu_custom_call" | custom-call | tf_op jit(solution)/shard_map/pallas_call | solution.py:85
  96.3 0.7 collective-permute-done.1.other_ref
  97.0 0.2 shard_map.168
  97.3 17.4 %all_to_all.27.parts_ref = bf16[8,112,512]{2,1,0:T(8,128)(2,1)S(1)} all-to-all(bf16[8,112,512]{2,1,0:T(8,128)(2,1)S(1)} %shard_map.168), channel_id=1, replica_groups={{0,16,32,48,64,80,96,112},{8,24,40,56,72,88,104,120},{1,17,33,49,65,81,..., dimensions={0} | all-to-all | bytes 1835008 | tf_op jit(solution)/shard_map/all_to_all | solution.py:599
  114.7 0.1 shard_map.169
  114.8 18.0 %all_to_all.28.parts_ref = bf16[8,112,512]{2,1,0:T(8,128)(2,1)S(1)} all-to-all(bf16[8,112,512]{2,1,0:T(8,128)(2,1)S(1)} %shard_map.169), channel_id=1, replica_groups=mesh['dp'=16,'graph'=8] {'graph'}, dimensions={0} | all-to-all | bytes 1835008 | tf_op jit(solution)/shard_map/all_to_all | solution.py:606
  132.7 0.7 shard_map.170
Async XLA Ops:
  2.5 23.3 %copy-start.1 = (bf16[1024,512]{1,0:T(8,128)(2,1)S(1)}, bf16[1024,512]{1,0:T(8,128)(2,1)}, u32[]{:S(2)}) copy-start(bf16[1024,512]{1,0:T(8,128)(2,1)} %feats_ref.3) | copy-start | bytes 3145732
  2.5 20.8 %all-to-all-start = ((bf16[8,112,512]{2,1,0:T(8,128)(2,1)}), bf16[8,112,512]{2,1,0:T(8,128)(2,1)S(1)}, u32[]{:S(2)}, u32[]{:S(2)}) async-start(bf16[8,112,512]{2,1,0:T(8,128)(2,1)} %shard_map.162), calls=%async_computation | async-start | bytes 1835008 | tf_op jit(solution)/shard_map/all_to_all | solution.py:552
  23.3 3.9 %copy-start = (bf16[8,112,512]{2,1,0:T(8,128)(2,1)}, bf16[8,112,512]{2,1,0:T(8,128)(2,1)S(1)}, u32[]{:S(2)}) copy-start(bf16[8,112,512]{2,1,0:T(8,128)(2,1)S(1)} %all-to-all-done.own_ref.refs_5_) | copy-start | bytes 2752516
  23.3 2.5 %collective-permute-start = (bf16[8,112,512]{2,1,0:T(8,128)(2,1)S(1)}, bf16[8,112,512]{2,1,0:T(8,128)(2,1)S(1)}, u32[]{:S(2)}, u32[]{:S(2)}) collective-permute-start(bf16[8,112,512]{2,1,0:T(8,128)(2,1)S(1)} %all-to-all-done.own_ref.refs_5_), channel_id=1, source_target_pairs={{0,8},{8,0},{16,24},{24,16},{32,40},{40,32},{48,56},{56,48},{64,72... | collective-permute-start | bytes 2752520 | tf_op jit(solution)/shard_map/ppermute | solution.py:535
  25.8 1.5 %copy-start.2 = (bf16[8,112,512]{2,1,0:T(8,128)(2,1)}, bf16[8,112,512]{2,1,0:T(8,128)(2,1)S(1)}, u32[]{:S(2)}) copy-start(bf16[8,112,512]{2,1,0:T(8,128)(2,1)S(1)} %collective-permute-done.other_ref.refs_6_) | copy-start | bytes 2752516
  71.7 20.0 %copy-start.3 = (bf16[8,64,512]{2,1,0:T(8,128)(2,1)S(1)}, bf16[8,64,512]{2,1,0:T(8,128)(2,1)}, u32[]{:S(2)}) copy-start(bf16[8,64,512]{2,1,0:T(8,128)(2,1)} %get-tuple-element.44.early_ref) | copy-start | bytes 1572868
  71.7 20.0 %copy-start.4 = (bf16[8,64,512]{2,1,0:T(8,128)(2,1)S(1)}, bf16[8,64,512]{2,1,0:T(8,128)(2,1)}, u32[]{:S(2)}) copy-start(bf16[8,64,512]{2,1,0:T(8,128)(2,1)} %get-tuple-element.45.early_other_ref) | copy-start | bytes 1572868
  71.7 20.0 %copy-start.5 = (f32[64,512]{1,0:T(8,128)S(1)}, f32[64,512]{1,0:T(8,128)}, u32[]{:S(2)}) copy-start(f32[64,512]{1,0:T(8,128)} %get-tuple-element.43.up_ref) | copy-start | bytes 393220
  91.6 0.7 copy-start.6
  94.5 2.6 %collective-permute-start.1 = (bf16[8,112,512]{2,1,0:T(8,128)(2,1)S(1)}, bf16[8,112,512]{2,1,0:T(8,128)(2,1)S(1)}, u32[]{:S(2)}, u32[]{:S(2)}) collective-permute-start(bf16[8,112,512]{2,1,0:T(8,128)(2,1)S(1)} %get-tuple-element.46), channel_id=1, source_target_pairs={{0,8},{8,0},{16,24},{24,16},{32,40},{40,32},{48,56},{56,48},{64,72... | collective-permute-start | bytes 2752520 | tf_op jit(solution)/shard_map/ppermute | solution.py:535

commit v3 on v2

--- a/solution.py
+++ b/solution.py
@@ -166,7 +166,6 @@
 
 
 def middle_kernel(
-    ready,
     slot_ref,
     core_ref,
     down_ref,
@@ -238,7 +237,6 @@
 
     lax.fori_loop(0, slots // width, forward, 0)
 
-    ready()
     w_first = w_first_s[...]
     w_second = w_second_s[...]
     for q in range(parts):
@@ -312,8 +310,7 @@
             pltpu.VMEM((lines, LANES), jnp.int32),
             pltpu.VMEM((slots // PIECE * (nb + 8), PIECE), F32),
         ],
-        hbm=(0, 1, 2),
-        vmem=60,
+        vmem=32,
     )
 
 
@@ -353,9 +350,7 @@
             vmem(down.shape, F32),
         ],
         smem=(0, 1),
-        hbm=(2, 3, 4, 5, 6),
-        lazy=(7,),
-        vmem=60,
+        vmem=44,
     )
 
 

time: 134 us -> 129 us (0.963)
  Pallas kernels: 36.6 us -> 31.6 us
  waiting for transfers between devices: 9.53 us -> 11.3 us
    pallas_call x9, Pallas kernels: 36.6 us -> 31.6 us  [call(): pl.pallas_call(body if fetched else kernel, out_shape=out_shape, in_specs...]
    all_to_all x1, waiting for transfers between devices: 6.31 us -> 8.11 us  [on_device(): own = lax.all_to_all(own, 'dp', 0, 0, axis_index_groups=same_core)]
  transfers between devices with their start and end apart: 3 -> 3, of which waited for: 3 -> 3; matrix products, arithmetic and copies ran while one was open for 0% -> 0% of each run, Pallas kernels for 7% -> 6%
where the time goes in v3:
time: 129 us
  blocking collectives  78.6 us (61%)
  Pallas kernels  31.6 us (24%)
  waiting for transfers between devices  11.3 us (9%)
  starting transfers between devices  6.56 us (5%)
    pallas_call x9, Pallas kernels, call(): pl.pallas_call(body if fetched else kernel, out_shape=out_shape, in_specs...  31.6 us
    all_to_all x1, blocking collectives, on_device(): down = lax.all_to_all(down, 'graph', 0, 0)  24.1 us
    all_to_all x1, blocking collectives, on_device(): parts = lax.all_to_all(partial, 'graph', 0, 0)  19.2 us
    all_to_all x1, blocking collectives, on_device(): sums = lax.all_to_all(sums, 'graph', 0, 0)  18 us
    all_to_all x1, blocking collectives, on_device(): chip = lax.all_to_all(chip, 'dp', 0, 0, axis_index_groups=same_core)  17.4 us
    all_to_all x1, waiting for transfers between devices, on_device(): own = lax.all_to_all(own, 'dp', 0, 0, axis_index_groups=same_core)  8.11 us
    all_to_all x1, starting transfers between devices, on_device(): own = lax.all_to_all(own, 'dp', 0, 0, axis_index_groups=same_core)  6.47 us
    ppermute x2, waiting for transfers between devices, swap(): lax.ppermute(value, 'dp', [(owner, owner ^ 1) for owner in range(owners)])  3.22 us
  transfers between devices with their start and end apart: 3, of which 3 were waited for; matrix products, arithmetic and copies ran while one was open for 0% of the time, Pallas kernels for 6%

profile of v3, /device:TPU:0, one launch (start us, length us, event | category | flops | bytes accessed | tf_op | source)
XLA Modules:
  0.0 128.9 jit_solution(8365509223441752578)
XLA Ops:
  0.6 1.9 %shard_map.162 = bf16[8,112,512]{2,1,0:T(8,128)(2,1)} custom-call(bf16[32,512]{1,0:T(8,128)(2,1)} %refs_0_.1, bf16[32,64]{1,0:T(8,128)(2,1)} %refs_1_.1, bf16[1,64]{1,0:T(2,128)(2,1)} %refs_2_.1, bf16[4,512]{1,0:T(4,128)(2,1)} %refs_3_.1, bf16[32,512]{1,0:T(8,128)(2,1)} %refs_4_.1, bf16[32,512]{1,0:T(8,128)(2,1)} %refs_5_.1), custom_call_target="tpu_custom_call" | custom-call | tf_op jit(solution)/shard_map/pallas_call | solution.py:85
  2.5 0.0 copy-start.2
  2.5 0.0 copy-start.3
  2.5 0.0 copy-start.4
  2.6 0.0 copy-start
  2.6 6.5 %all-to-all-start = ((bf16[8,112,512]{2,1,0:T(8,128)(2,1)}), bf16[8,112,512]{2,1,0:T(8,128)(2,1)S(1)}, u32[]{:S(2)}, u32[]{:S(2)}) async-start(bf16[8,112,512]{2,1,0:T(8,128)(2,1)} %shard_map.162), calls=%async_computation | async-start | bytes 1835008 | tf_op jit(solution)/shard_map/all_to_all | solution.py:547
  9.0 0.0 copy-done.2
  9.0 0.0 copy-done.3
  9.1 0.0 copy-done.4
  9.1 6.2 %shard_map.163 = (s32[8,10240]{1,0:T(8,128)S(1)}, bf16[16,10240]{1,0:T(8,128)(2,1)S(1)}, s32[1,128]{1,0:T(1,128)S(1)}) custom-call(s32[64,128]{1,0:T(8,128)S(1)} %bitcast.3, s32[64,128]{1,0:T(8,128)S(1)} %bitcast.4, bf16[16,8192]{1,0:T(8,128)(2,1)S(1)} %copy-done.2), custom_call_target="tpu_custom_call" | custom-call | tf_op jit(solution)/shard_map/pallas_call | solution.py:85
  15.2 8.1 %all-to-all-done.own_ref = bf16[8,112,512]{2,1,0:T(8,128)(2,1)S(1)} async-done(((bf16[8,112,512]{2,1,0:T(8,128)(2,1)}), bf16[8,112,512]{2,1,0:T(8,128)(2,1)S(1)}, u32[]{:S(2)}, u32[]{:S(2)}) %all-to-all-start) | async-done | bytes 917536 | tf_op jit(solution)/shard_map/all_to_all | solution.py:547
  23.3 0.0 collective-permute-start
  23.3 2.5 %collective-permute-done.other_ref = bf16[8,112,512]{2,1,0:T(8,128)(2,1)S(1)} collective-permute-done((bf16[8,112,512]{2,1,0:T(8,128)(2,1)S(1)}, bf16[8,112,512]{2,1,0:T(8,128)(2,1)S(1)}, u32[]{:S(2)}, u32[]{:S(2)}) %collective-permute-start) | collective-permute-done | bytes 917536 | tf_op jit(solution)/shard_map/ppermute | solution.py:530
  25.8 0.0 copy-done
  25.8 1.4 %shard_map.164 = (bf16[8,256,256]{2,1,0:T(8,128)(2,1)S(1)}, bf16[512,640]{1,0:T(8,128)(2,1)S(1)}) custom-call(s32[1]{0:T(128)} %bitcast.core_ref, bf16[1024,512]{1,0:T(8,128)(2,1)S(1)} %copy-done, bf16[8,112,512]{2,1,0:T(8,128)(2,1)S(1)} %all-to-all-done.own_ref, bf16[8,112,512]{2,1,0:T(8,128)(2,1)S(1)} %collective-permute-done.other_ref), custom_call_target="tpu_custom_call" | custom-call | tf_op jit(solution)/shard_map/pallas_call | solution.py:85
  27.3 0.0 copy-start.1
  27.3 24.1 %all_to_all.25.down_ref = bf16[8,256,256]{2,1,0:T(8,128)(2,1)S(1)} all-to-all(bf16[8,256,256]{2,1,0:T(8,128)(2,1)S(1)} %get-tuple-element.37), channel_id=1, replica_groups=mesh['dp'=16,'graph'=8] {'graph'}, dimensions={0} | all-to-all | bytes 2097152 | tf_op jit(solution)/shard_map/all_to_all | solution.py:564
  51.3 0.0 copy-done.1
  51.3 17.1 %shard_map.165 = (bf16[8,256,256]{2,1,0:T(8,128)(2,1)S(1)}, bf16[8,64,512]{2,1,0:T(8,128)(2,1)S(1)}, bf16[8,64,512]{2,1,0:T(8,128)(2,1)S(1)}, f32[64,512]{1,0:T(8,128)S(1)}, f32[16,64]{1,0:T(8,128)S(1)}) custom-call(s32[1,128]{1,0:T(1,128)S(1)} %get-tuple-element.33.slot_ref, s32[1]{0:T(128)} %bitcast.core_ref, ...), custom_call_target="tpu_custom_call" | custom-call | tf_op jit(solution)/shard_map/pallas_call | solution.py:85
  68.5 19.2 %all_to_all.26.parts_ref = bf16[8,256,256]{2,1,0:T(8,128)(2,1)S(1)} all-to-all(bf16[8,256,256]{2,1,0:T(8,128)(2,1)S(1)} %get-tuple-element.40), channel_id=1, replica_groups=mesh['dp'=16,'graph'=8] {'graph'}, dimensions={0} | all-to-all | bytes 2097152 | tf_op jit(solution)/shard_map/all_to_all | solution.py:568
  87.7 2.1 %shard_map.166 = (bf16[1024,512]{1,0:T(8,128)(2,1)S(1)}, bf16[8,112,512]{2,1,0:T(8,128)(2,1)S(1)}, bf16[8,112,512]{2,1,0:T(8,128)(2,1)S(1)}) custom-call(s32[1]{0:T(128)} %bitcast.core_ref, bf16[8,256,256]{2,1,0:T(8,128)(2,1)S(1)} %all_to_all.26.parts_ref, bf16[1024,512]{1,0:T(8,128)(2,1)S(1)} %copy-done, ...), custom_call_target="tpu_custom_call" | custom-call | tf_op jit(solution)/shard_map/pallas_call | solution.py:85
  89.9 0.1 collective-permute-start.1
  90.0 1.7 %shard_map.167 = bf16[1024,512]{1,0:T(8,128)(2,1)} custom-call(bf16[1024,512]{1,0:T(8,128)(2,1)S(1)} %get-tuple-element.47.dz_ref, bf16[512,640]{1,0:T(8,128)(2,1)S(1)} %get-tuple-element.41.weights_ref), custom_call_target="tpu_custom_call" | custom-call | tf_op jit(solution)/shard_map/pallas_call | solution.py:85
  91.7 0.7 collective-permute-done.1.other_ref
  92.4 0.2 shard_map.168
  92.6 17.4 %all_to_all.27.parts_ref = bf16[8,112,512]{2,1,0:T(8,128)(2,1)S(1)} all-to-all(bf16[8,112,512]{2,1,0:T(8,128)(2,1)S(1)} %shard_map.168), channel_id=1, replica_groups={{0,16,32,48,64,80,96,112},{8,24,40,56,72,88,104,120},{1,17,33,49,65,81,..., dimensions={0} | all-to-all | bytes 1835008 | tf_op jit(solution)/shard_map/all_to_all | solution.py:594
  110.0 0.1 shard_map.169
  110.2 18.0 %all_to_all.28.parts_ref = bf16[8,112,512]{2,1,0:T(8,128)(2,1)S(1)} all-to-all(bf16[8,112,512]{2,1,0:T(8,128)(2,1)S(1)} %shard_map.169), channel_id=1, replica_groups=mesh['dp'=16,'graph'=8] {'graph'}, dimensions={0} | all-to-all | bytes 1835008 | tf_op jit(solution)/shard_map/all_to_all | solution.py:601
  128.1 0.7 shard_map.170
Async XLA Ops:
  2.5 6.5 %copy-start.2 = (bf16[16,8192]{1,0:T(8,128)(2,1)S(1)}, bf16[16,8192]{1,0:T(8,128)(2,1)}, u32[]{:S(2)}) copy-start(bf16[16,8192]{1,0:T(8,128)(2,1)} %basis_ref.1) | copy-start | bytes 786436
  2.5 6.5 %copy-start.3 = (s32[8192]{0:T(1024)S(1)}, s32[8192]{0:T(1024)}, u32[]{:S(2)}) copy-start(s32[8192]{0:T(1024)} %param.14) | copy-start | bytes 98308
  2.5 6.5 %copy-start.4 = (s32[8192]{0:T(1024)S(1)}, s32[8192]{0:T(1024)}, u32[]{:S(2)}) copy-start(s32[8192]{0:T(1024)} %param.15) | copy-start | bytes 98308
  2.6 23.3 %copy-start = (bf16[1024,512]{1,0:T(8,128)(2,1)S(1)}, bf16[1024,512]{1,0:T(8,128)(2,1)}, u32[]{:S(2)}) copy-start(bf16[1024,512]{1,0:T(8,128)(2,1)} %feats_ref.3) | copy-start | bytes 3145732
  2.6 20.8 %all-to-all-start = ((bf16[8,112,512]{2,1,0:T(8,128)(2,1)}), bf16[8,112,512]{2,1,0:T(8,128)(2,1)S(1)}, u32[]{:S(2)}, u32[]{:S(2)}) async-start(bf16[8,112,512]{2,1,0:T(8,128)(2,1)} %shard_map.162), calls=%async_computation | async-start | bytes 1835008 | tf_op jit(solution)/shard_map/all_to_all | solution.py:547
  23.3 2.5 %collective-permute-start = (bf16[8,112,512]{2,1,0:T(8,128)(2,1)S(1)}, bf16[8,112,512]{2,1,0:T(8,128)(2,1)S(1)}, u32[]{:S(2)}, u32[]{:S(2)}) collective-permute-start(bf16[8,112,512]{2,1,0:T(8,128)(2,1)S(1)} %all-to-all-done.own_ref), channel_id=1, source_target_pairs={{0,8},{8,0},{16,24},{24,16},{32,40},{40,32},{48,56},{56,48},{64,72... | collective-permute-start | bytes 2752520 | tf_op jit(solution)/shard_map/ppermute | solution.py:530
  27.3 24.1 %copy-start.1 = (bf16[1024,512]{1,0:T(8,128)(2,1)S(1)}, bf16[1024,512]{1,0:T(8,128)(2,1)}, u32[]{:S(2)}) copy-start(bf16[1024,512]{1,0:T(8,128)(2,1)} %cot_ref.1) | copy-start | bytes 3145732
  89.9 2.6 %collective-permute-start.1 = (bf16[8,112,512]{2,1,0:T(8,128)(2,1)S(1)}, bf16[8,112,512]{2,1,0:T(8,128)(2,1)S(1)}, u32[]{:S(2)}, u32[]{:S(2)}) collective-permute-start(bf16[8,112,512]{2,1,0:T(8,128)(2,1)S(1)} %get-tuple-element.46), channel_id=1, source_target_pairs={{0,8},{8,0},{16,24},{24,16},{32,40},{40,32},{48,56},{56,48},{64,72... | collective-permute-start | bytes 2752520 | tf_op jit(solution)/shard_map/ppermute | solution.py:530

commit v4 on v3

--- a/solution.py
+++ b/solution.py
@@ -16,7 +16,8 @@
 LANES = 128
 SMALL_ROWS = 16
 CHUNK = 256
-GROUP = 20
+GROUP = 40
+SPAN = 2048
 LINES = 16
 PIECE = 512
 MIB = 1024 * 1024
@@ -219,20 +220,23 @@
     agg_acc[...] = jnp.zeros_like(agg_acc)
 
     def forward(step, carry):
-        cols = pl.ds(pl.multiple_of(step * width, width), width)
-        found = []
-        for k in range(GROUP):
-            here = pl.ds(pl.multiple_of(step * width + k * CHUNK, CHUNK), CHUNK)
-            slot = slot_ref[0, step * GROUP + k]
-            hot = one_hot(rows_ref[0:1, here], e_hi)
-            found.append(pick(dot(down_ref[slot], hot), rows_ref[1:2, here], parts))
-        down_in = jnp.concatenate(found, axis=1)
-        coeff = dot(w_basis, basis_ref[:, cols])
-        down_in_s[:, cols] = down_in.astype(BF16)
-        coeff_s[:, cols] = coeff
-        hot_e = one_hot(rows_ref[2:3, cols], e_hi)
-        placed = spread(down_in * coeff, rows_ref[3:4, cols], parts)
-        agg_acc[...] += dot(hot_e, placed, NT)
+        total_agg = agg_acc[...]
+        for first in range(0, width, SPAN):
+            cols = pl.ds(pl.multiple_of(step * width + first, SPAN), SPAN)
+            found = []
+            for k in range(first // CHUNK, (first + SPAN) // CHUNK):
+                here = pl.ds(pl.multiple_of(step * width + k * CHUNK, CHUNK), CHUNK)
+                slot = slot_ref[0, step * GROUP + k]
+                hot = one_hot(rows_ref[0:1, here], e_hi)
+                found.append(pick(dot(down_ref[slot], hot), rows_ref[1:2, here], parts))
+            down_in = jnp.concatenate(found, axis=1)
+            coeff = dot(w_basis, basis_ref[:, cols])
+            down_in_s[:, cols] = down_in.astype(BF16)
+            coeff_s[:, cols] = coeff
+            hot_e = one_hot(rows_ref[2:3, cols], e_hi)
+            placed = spread(down_in * coeff, rows_ref[3:4, cols], parts)
+            total_agg += dot(hot_e, placed, NT)
+        agg_acc[...] = total_agg
         return carry
 
     lax.fori_loop(0, slots // width, forward, 0)
@@ -275,19 +279,20 @@
     total[...] = jnp.zeros_like(total)
 
     def backward(step, carry):
-        cols = pl.ds(pl.multiple_of(step * width, width), width)
-        hot_e = one_hot(rows_ref[2:3, cols], e_hi)
-        dagg_out = pick(dot(dagg_s[...], hot_e), rows_ref[3:4, cols], parts)
-        dcoeff = (dagg_out * down_in_s[:, cols].astype(F32)).astype(BF16)
-        basis_grad_ref[...] += dot(basis_ref[:, cols], dcoeff, NT)
-        placed = spread(dagg_out * coeff_s[:, cols], rows_ref[1:2, cols], parts)
-        hot = one_hot(rows_ref[0:1, cols], e_hi)
-        terms = []
-        for k in range(GROUP):
-            here = slice(k * CHUNK, (k + 1) * CHUNK)
-            terms.append(dot(placed[:, here], hot[:, here], NT))
-        for k in range(GROUP):
-            total[slot_ref[0, step * GROUP + k]] += terms[k]
+        total_basis = basis_grad_ref[...]
+        for first in range(0, width, SPAN):
+            cols = pl.ds(pl.multiple_of(step * width + first, SPAN), SPAN)
+            hot_e = one_hot(rows_ref[2:3, cols], e_hi)
+            dagg_out = pick(dot(dagg_s[...], hot_e), rows_ref[3:4, cols], parts)
+            dcoeff = (dagg_out * down_in_s[:, cols].astype(F32)).astype(BF16)
+            total_basis += dot(basis_ref[:, cols], dcoeff, NT)
+            placed = spread(dagg_out * coeff_s[:, cols], rows_ref[1:2, cols], parts)
+            hot = one_hot(rows_ref[0:1, cols], e_hi)
+            for k in range(SPAN // CHUNK):
+                here = slice(k * CHUNK, (k + 1) * CHUNK)
+                slot = slot_ref[0, step * GROUP + first // CHUNK + k]
+                total[slot] += dot(placed[:, here], hot[:, here], NT)
+        basis_grad_ref[...] = total_basis
         return carry
 
     lax.fori_loop(0, slots // width, backward, 0)

time: 129 us -> 126 us (0.977)
  Pallas kernels: 31.6 us -> 27.7 us
    pallas_call x9, Pallas kernels: 31.6 us -> 27.7 us  [call(): pl.pallas_call(body if fetched else kernel, out_shape=out_shape, in_specs...]
where the time goes in v4:
time: 126 us; the launch traced here: 125 us
  blocking collectives  78.9 us (63%)
  Pallas kernels  27.7 us (22%)
  waiting for transfers between devices  11.3 us (9%)
  starting transfers between devices  6.56 us (5%)
    pallas_call x9, Pallas kernels, call(): pl.pallas_call(body if fetched else kernel, out_shape=out_shape, in_specs...  27.7 us
    all_to_all x1, blocking collectives, on_device(): down = lax.all_to_all(down, 'graph', 0, 0)  24.1 us
    all_to_all x1, blocking collectives, on_device(): parts = lax.all_to_all(partial, 'graph', 0, 0)  19.5 us
    all_to_all x1, blocking collectives, on_device(): sums = lax.all_to_all(sums, 'graph', 0, 0)  18 us
    all_to_all x1, blocking collectives, on_device(): chip = lax.all_to_all(chip, 'dp', 0, 0, axis_index_groups=same_core)  17.4 us
    all_to_all x1, waiting for transfers between devices, on_device(): own = lax.all_to_all(own, 'dp', 0, 0, axis_index_groups=same_core)  8.11 us
    all_to_all x1, starting transfers between devices, on_device(): own = lax.all_to_all(own, 'dp', 0, 0, axis_index_groups=same_core)  6.47 us
    ppermute x2, waiting for transfers between devices, swap(): lax.ppermute(value, 'dp', [(owner, owner ^ 1) for owner in range(owners)])  3.22 us
  transfers between devices with their start and end apart: 3, of which 3 were waited for; matrix products, arithmetic and copies ran while one was open for 0% of the time, Pallas kernels for 6%

profile of v4, /device:TPU:0, one launch (start us, length us, event | category | flops | bytes accessed | tf_op | source)
XLA Modules:
  0.0 125.3 jit_solution(16290151381657985028)
XLA Ops:
  0.6 1.9 %shard_map.162 = bf16[8,112,512]{2,1,0:T(8,128)(2,1)} custom-call(bf16[32,512]{1,0:T(8,128)(2,1)} %refs_0_.1, bf16[32,64]{1,0:T(8,128)(2,1)} %refs_1_.1, bf16[1,64]{1,0:T(2,128)(2,1)} %refs_2_.1, bf16[4,512]{1,0:T(4,128)(2,1)} %refs_3_.1, bf16[32,512]{1,0:T(8,128)(2,1)} %refs_4_.1, bf16[32,512]{1,0:T(8,128)(2,1)} %refs_5_.1), custom_call_target="tpu_custom_call" | custom-call | tf_op jit(solution)/shard_map/pallas_call | solution.py:86
  2.5 0.0 copy-start.2
  2.5 0.0 copy-start.3
  2.5 0.0 copy-start.4
  2.6 0.0 copy-start
  2.6 6.5 %all-to-all-start = ((bf16[8,112,512]{2,1,0:T(8,128)(2,1)}), bf16[8,112,512]{2,1,0:T(8,128)(2,1)S(1)}, u32[]{:S(2)}, u32[]{:S(2)}) async-start(bf16[8,112,512]{2,1,0:T(8,128)(2,1)} %shard_map.162), calls=%async_computation | async-start | bytes 1835008 | tf_op jit(solution)/shard_map/all_to_all | solution.py:552
  9.0 0.0 copy-done.2
  9.0 0.0 copy-done.3
  9.1 0.0 copy-done.4
  9.1 6.2 %shard_map.163 = (s32[8,10240]{1,0:T(8,128)S(1)}, bf16[16,10240]{1,0:T(8,128)(2,1)S(1)}, s32[1,128]{1,0:T(1,128)S(1)}) custom-call(s32[64,128]{1,0:T(8,128)S(1)} %bitcast.3, s32[64,128]{1,0:T(8,128)S(1)} %bitcast.4, bf16[16,8192]{1,0:T(8,128)(2,1)S(1)} %copy-done.2), custom_call_target="tpu_custom_call" | custom-call | tf_op jit(solution)/shard_map/pallas_call | solution.py:86
  15.2 8.1 %all-to-all-done.own_ref = bf16[8,112,512]{2,1,0:T(8,128)(2,1)S(1)} async-done(((bf16[8,112,512]{2,1,0:T(8,128)(2,1)}), bf16[8,112,512]{2,1,0:T(8,128)(2,1)S(1)}, u32[]{:S(2)}, u32[]{:S(2)}) %all-to-all-start) | async-done | bytes 917536 | tf_op jit(solution)/shard_map/all_to_all | solution.py:552
  23.3 0.0 collective-permute-start
  23.3 2.5 %collective-permute-done.other_ref = bf16[8,112,512]{2,1,0:T(8,128)(2,1)S(1)} collective-permute-done((bf16[8,112,512]{2,1,0:T(8,128)(2,1)S(1)}, bf16[8,112,512]{2,1,0:T(8,128)(2,1)S(1)}, u32[]{:S(2)}, u32[]{:S(2)}) %collective-permute-start) | collective-permute-done | bytes 917536 | tf_op jit(solution)/shard_map/ppermute | solution.py:535
  25.8 0.0 copy-done
  25.8 1.4 %shard_map.164 = (bf16[8,256,256]{2,1,0:T(8,128)(2,1)S(1)}, bf16[512,640]{1,0:T(8,128)(2,1)S(1)}) custom-call(s32[1]{0:T(128)} %bitcast.core_ref, bf16[1024,512]{1,0:T(8,128)(2,1)S(1)} %copy-done, bf16[8,112,512]{2,1,0:T(8,128)(2,1)S(1)} %all-to-all-done.own_ref, bf16[8,112,512]{2,1,0:T(8,128)(2,1)S(1)} %collective-permute-done.other_ref), custom_call_target="tpu_custom_call" | custom-call | tf_op jit(solution)/shard_map/pallas_call | solution.py:86
  27.3 0.0 copy-start.1
  27.3 24.1 %all_to_all.25.down_ref = bf16[8,256,256]{2,1,0:T(8,128)(2,1)S(1)} all-to-all(bf16[8,256,256]{2,1,0:T(8,128)(2,1)S(1)} %get-tuple-element.37), channel_id=1, replica_groups=mesh['dp'=16,'graph'=8] {'graph'}, dimensions={0} | all-to-all | bytes 2097152 | tf_op jit(solution)/shard_map/all_to_all | solution.py:569
  51.3 0.0 copy-done.1
  51.3 13.3 %shard_map.165 = (bf16[8,256,256]{2,1,0:T(8,128)(2,1)S(1)}, bf16[8,64,512]{2,1,0:T(8,128)(2,1)S(1)}, bf16[8,64,512]{2,1,0:T(8,128)(2,1)S(1)}, f32[64,512]{1,0:T(8,128)S(1)}, f32[16,64]{1,0:T(8,128)S(1)}) custom-call(s32[1,128]{1,0:T(1,128)S(1)} %get-tuple-element.33.slot_ref, s32[1]{0:T(128)} %bitcast.core_ref, ...), custom_call_target="tpu_custom_call" | custom-call | tf_op jit(solution)/shard_map/pallas_call | solution.py:86
  64.7 19.5 %all_to_all.26.parts_ref = bf16[8,256,256]{2,1,0:T(8,128)(2,1)S(1)} all-to-all(bf16[8,256,256]{2,1,0:T(8,128)(2,1)S(1)} %get-tuple-element.40), channel_id=1, replica_groups=mesh['dp'=16,'graph'=8] {'graph'}, dimensions={0} | all-to-all | bytes 2097152 | tf_op jit(solution)/shard_map/all_to_all | solution.py:573
  84.1 2.1 %shard_map.166 = (bf16[1024,512]{1,0:T(8,128)(2,1)S(1)}, bf16[8,112,512]{2,1,0:T(8,128)(2,1)S(1)}, bf16[8,112,512]{2,1,0:T(8,128)(2,1)S(1)}) custom-call(s32[1]{0:T(128)} %bitcast.core_ref, bf16[8,256,256]{2,1,0:T(8,128)(2,1)S(1)} %all_to_all.26.parts_ref, bf16[1024,512]{1,0:T(8,128)(2,1)S(1)} %copy-done, ...), custom_call_target="tpu_custom_call" | custom-call | tf_op jit(solution)/shard_map/pallas_call | solution.py:86
  86.3 0.1 collective-permute-start.1
  86.4 1.7 %shard_map.167 = bf16[1024,512]{1,0:T(8,128)(2,1)} custom-call(bf16[1024,512]{1,0:T(8,128)(2,1)S(1)} %get-tuple-element.47.dz_ref, bf16[512,640]{1,0:T(8,128)(2,1)S(1)} %get-tuple-element.41.weights_ref), custom_call_target="tpu_custom_call" | custom-call | tf_op jit(solution)/shard_map/pallas_call | solution.py:86
  88.1 0.8 collective-permute-done.1.other_ref
  88.8 0.2 shard_map.168
  89.0 17.4 %all_to_all.27.parts_ref = bf16[8,112,512]{2,1,0:T(8,128)(2,1)S(1)} all-to-all(bf16[8,112,512]{2,1,0:T(8,128)(2,1)S(1)} %shard_map.168), channel_id=1, replica_groups={{0,16,32,48,64,80,96,112},{8,24,40,56,72,88,104,120},{1,17,33,49,65,81,..., dimensions={0} | all-to-all | bytes 1835008 | tf_op jit(solution)/shard_map/all_to_all | solution.py:599
  106.4 0.1 shard_map.169
  106.6 18.0 %all_to_all.28.parts_ref = bf16[8,112,512]{2,1,0:T(8,128)(2,1)S(1)} all-to-all(bf16[8,112,512]{2,1,0:T(8,128)(2,1)S(1)} %shard_map.169), channel_id=1, replica_groups=mesh['dp'=16,'graph'=8] {'graph'}, dimensions={0} | all-to-all | bytes 1835008 | tf_op jit(solution)/shard_map/all_to_all | solution.py:606
  124.5 0.7 shard_map.170
Async XLA Ops:
  2.5 6.5 %copy-start.2 = (bf16[16,8192]{1,0:T(8,128)(2,1)S(1)}, bf16[16,8192]{1,0:T(8,128)(2,1)}, u32[]{:S(2)}) copy-start(bf16[16,8192]{1,0:T(8,128)(2,1)} %basis_ref.1) | copy-start | bytes 786436
  2.5 6.5 %copy-start.3 = (s32[8192]{0:T(1024)S(1)}, s32[8192]{0:T(1024)}, u32[]{:S(2)}) copy-start(s32[8192]{0:T(1024)} %param.14) | copy-start | bytes 98308
  2.5 6.5 %copy-start.4 = (s32[8192]{0:T(1024)S(1)}, s32[8192]{0:T(1024)}, u32[]{:S(2)}) copy-start(s32[8192]{0:T(1024)} %param.15) | copy-start | bytes 98308
  2.6 23.3 %copy-start = (bf16[1024,512]{1,0:T(8,128)(2,1)S(1)}, bf16[1024,512]{1,0:T(8,128)(2,1)}, u32[]{:S(2)}) copy-start(bf16[1024,512]{1,0:T(8,128)(2,1)} %feats_ref.3) | copy-start | bytes 3145732
  2.6 20.8 %all-to-all-start = ((bf16[8,112,512]{2,1,0:T(8,128)(2,1)}), bf16[8,112,512]{2,1,0:T(8,128)(2,1)S(1)}, u32[]{:S(2)}, u32[]{:S(2)}) async-start(bf16[8,112,512]{2,1,0:T(8,128)(2,1)} %shard_map.162), calls=%async_computation | async-start | bytes 1835008 | tf_op jit(solution)/shard_map/all_to_all | solution.py:552
  23.3 2.5 %collective-permute-start = (bf16[8,112,512]{2,1,0:T(8,128)(2,1)S(1)}, bf16[8,112,512]{2,1,0:T(8,128)(2,1)S(1)}, u32[]{:S(2)}, u32[]{:S(2)}) collective-permute-start(bf16[8,112,512]{2,1,0:T(8,128)(2,1)S(1)} %all-to-all-done.own_ref), channel_id=1, source_target_pairs={{0,8},{8,0},{16,24},{24,16},{32,40},{40,32},{48,56},{56,48},{64,72... | collective-permute-start | bytes 2752520 | tf_op jit(solution)/shard_map/ppermute | solution.py:535
  27.3 24.1 %copy-start.1 = (bf16[1024,512]{1,0:T(8,128)(2,1)S(1)}, bf16[1024,512]{1,0:T(8,128)(2,1)}, u32[]{:S(2)}) copy-start(bf16[1024,512]{1,0:T(8,128)(2,1)} %cot_ref.1) | copy-start | bytes 3145732
  86.3 2.6 %collective-permute-start.1 = (bf16[8,112,512]{2,1,0:T(8,128)(2,1)S(1)}, bf16[8,112,512]{2,1,0:T(8,128)(2,1)S(1)}, u32[]{:S(2)}, u32[]{:S(2)}) collective-permute-start(bf16[8,112,512]{2,1,0:T(8,128)(2,1)S(1)} %get-tuple-element.46), channel_id=1, source_target_pairs={{0,8},{8,0},{16,24},{24,16},{32,40},{40,32},{48,56},{56,48},{64,72... | collective-permute-start | bytes 2752520 | tf_op jit(solution)/shard_map/ppermute | solution.py:535

commit v5 on v4

--- a/solution.py
+++ b/solution.py
@@ -484,6 +484,11 @@
     for owner in range(1, parts_ref.shape[0]):
         total += parts_ref[owner].astype(F32)
     total = total.astype(BF16)
+    out_ref[...] = total
+
+
+def pair_sum_kernel(own_ref, other_ref, out_ref):
+    total = (own_ref[...].astype(F32) + other_ref[...].astype(F32)).astype(BF16)
     for peer in range(out_ref.shape[0]):
         out_ref[peer] = total
 
@@ -598,12 +603,14 @@
     chip = call(chip_sum_kernel, half, grads, other, vmem=16)
     chip = lax.all_to_all(chip, "dp", 0, 0, axis_index_groups=same_core)
     sums = call(
-        owners_sum_kernel,
-        shape((peers, 3 * share + SMALL_ROWS, width), BF16),
-        chip,
-        vmem=16,
-    )
-    sums = lax.all_to_all(sums, "graph", 0, 0)
+        owners_sum_kernel, shape((3 * share + SMALL_ROWS, width), BF16), chip, vmem=16
+    )
+    opposite = lax.ppermute(sums, "graph", [(peer, peer ^ 1) for peer in range(peers)])
+    sums = call(
+        pair_sum_kernel, shape((peers // 2,) + sums.shape, BF16), sums, opposite, vmem=16
+    )
+    along_y = [[2 * peer + side for peer in range(peers // 2)] for side in range(2)]
+    sums = lax.all_to_all(sums, "graph", 0, 0, axis_index_groups=along_y)
     pair, down_grad, basis_grad, up, first, second = call(
         peers_sum_kernel,
         (

time: 126 us -> 124 us (0.984)
  blocking collectives: 78.9 us -> 71 us
  waiting for transfers between devices: 11.3 us -> 16.8 us
    all_to_all x1, blocking collectives: 18 us -> 10.1 us  [on_device(): sums = lax.all_to_all(sums, 'graph', 0, 0, axis_index_groups=along_y)]
    ppermute x0 -> x1, waiting for transfers between devices: none -> 5.44 us  [on_device(): lax.ppermute(sums, 'graph', [(peer, peer ^ 1) for peer in range(peers)])]
    pallas_call x9 -> x10, Pallas kernels: 27.7 us -> 27.7 us  [call(): pl.pallas_call(body if fetched else kernel, out_shape=out_shape, in_specs...]
  transfers between devices with their start and end apart: 3 -> 4, of which waited for: 3 -> 4; matrix products, arithmetic and copies ran while one was open for 0% -> 0% of each run, Pallas kernels for 6% -> 6%
where the time goes in v5:
time: 124 us
  blocking collectives  71 us (57%)
  Pallas kernels  27.7 us (22%)
  waiting for transfers between devices  16.8 us (14%)
  starting transfers between devices  7.49 us (6%)
    pallas_call x10, Pallas kernels, call(): pl.pallas_call(body if fetched else kernel, out_shape=out_shape, in_specs...  27.7 us
    all_to_all x1, blocking collectives, on_device(): down = lax.all_to_all(down, 'graph', 0, 0)  24.1 us
    all_to_all x1, blocking collectives, on_device(): parts = lax.all_to_all(partial, 'graph', 0, 0)  19.5 us
    all_to_all x1, blocking collectives, on_device(): chip = lax.all_to_all(chip, 'dp', 0, 0, axis_index_groups=same_core)  17.4 us
    all_to_all x1, blocking collectives, on_device(): sums = lax.all_to_all(sums, 'graph', 0, 0, axis_index_groups=along_y)  10.1 us
    all_to_all x1, waiting for transfers between devices, on_device(): own = lax.all_to_all(own, 'dp', 0, 0, axis_index_groups=same_core)  8.11 us
    all_to_all x1, starting transfers between devices, on_device(): own = lax.all_to_all(own, 'dp', 0, 0, axis_index_groups=same_core)  6.47 us
    ppermute x1, waiting for transfers between devices, on_device(): lax.ppermute(sums, 'graph', [(peer, peer ^ 1) for peer in range(peers)])  5.44 us
  transfers between devices with their start and end apart: 4, of which 4 were waited for; matrix products, arithmetic and copies ran while one was open for 0% of the time, Pallas kernels for 6%

profile of v5, /device:TPU:0, one launch (start us, length us, event | category | flops | bytes accessed | tf_op | source)
XLA Modules:
  0.0 123.8 jit_solution(4195190057925296536)
XLA Ops:
  0.6 1.9 %shard_map.162 = bf16[8,112,512]{2,1,0:T(8,128)(2,1)} custom-call(bf16[32,512]{1,0:T(8,128)(2,1)} %refs_0_.1, bf16[32,64]{1,0:T(8,128)(2,1)} %refs_1_.1, bf16[1,64]{1,0:T(2,128)(2,1)} %refs_2_.1, bf16[4,512]{1,0:T(4,128)(2,1)} %refs_3_.1, bf16[32,512]{1,0:T(8,128)(2,1)} %refs_4_.1, bf16[32,512]{1,0:T(8,128)(2,1)} %refs_5_.1), custom_call_target="tpu_custom_call" | custom-call | tf_op jit(solution)/shard_map/pallas_call | solution.py:86
  2.5 0.0 copy-start.2
  2.5 0.0 copy-start.3
  2.5 0.0 copy-start.4
  2.6 0.0 copy-start
  2.6 6.5 %all-to-all-start = ((bf16[8,112,512]{2,1,0:T(8,128)(2,1)}), bf16[8,112,512]{2,1,0:T(8,128)(2,1)S(1)}, u32[]{:S(2)}, u32[]{:S(2)}) async-start(bf16[8,112,512]{2,1,0:T(8,128)(2,1)} %shard_map.162), calls=%async_computation | async-start | bytes 1835008 | tf_op jit(solution)/shard_map/all_to_all | solution.py:557
  9.0 0.0 copy-done.2
  9.0 0.0 copy-done.3
  9.1 0.0 copy-done.4
  9.1 6.2 %shard_map.163 = (s32[8,10240]{1,0:T(8,128)S(1)}, bf16[16,10240]{1,0:T(8,128)(2,1)S(1)}, s32[1,128]{1,0:T(1,128)S(1)}) custom-call(s32[64,128]{1,0:T(8,128)S(1)} %bitcast.3, s32[64,128]{1,0:T(8,128)S(1)} %bitcast.4, bf16[16,8192]{1,0:T(8,128)(2,1)S(1)} %copy-done.2), custom_call_target="tpu_custom_call" | custom-call | tf_op jit(solution)/shard_map/pallas_call | solution.py:86
  15.2 8.1 %all-to-all-done.own_ref = bf16[8,112,512]{2,1,0:T(8,128)(2,1)S(1)} async-done(((bf16[8,112,512]{2,1,0:T(8,128)(2,1)}), bf16[8,112,512]{2,1,0:T(8,128)(2,1)S(1)}, u32[]{:S(2)}, u32[]{:S(2)}) %all-to-all-start) | async-done | bytes 917536 | tf_op jit(solution)/shard_map/all_to_all | solution.py:557
  23.3 0.0 collective-permute-start
  23.3 2.5 %collective-permute-done.other_ref = bf16[8,112,512]{2,1,0:T(8,128)(2,1)S(1)} collective-permute-done((bf16[8,112,512]{2,1,0:T(8,128)(2,1)S(1)}, bf16[8,112,512]{2,1,0:T(8,128)(2,1)S(1)}, u32[]{:S(2)}, u32[]{:S(2)}) %collective-permute-start) | collective-permute-done | bytes 917536 | tf_op jit(solution)/shard_map/ppermute | solution.py:540
  25.8 0.0 copy-done
  25.8 1.4 %shard_map.164 = (bf16[8,256,256]{2,1,0:T(8,128)(2,1)S(1)}, bf16[512,640]{1,0:T(8,128)(2,1)S(1)}) custom-call(s32[1]{0:T(128)} %bitcast.core_ref, bf16[1024,512]{1,0:T(8,128)(2,1)S(1)} %copy-done, bf16[8,112,512]{2,1,0:T(8,128)(2,1)S(1)} %all-to-all-done.own_ref, bf16[8,112,512]{2,1,0:T(8,128)(2,1)S(1)} %collective-permute-done.other_ref), custom_call_target="tpu_custom_call" | custom-call | tf_op jit(solution)/shard_map/pallas_call | solution.py:86
  27.3 0.0 copy-start.1
  27.3 24.1 %all_to_all.25.down_ref = bf16[8,256,256]{2,1,0:T(8,128)(2,1)S(1)} all-to-all(bf16[8,256,256]{2,1,0:T(8,128)(2,1)S(1)} %get-tuple-element.37), channel_id=1, replica_groups=mesh['dp'=16,'graph'=8] {'graph'}, dimensions={0} | all-to-all | bytes 2097152 | tf_op jit(solution)/shard_map/all_to_all | solution.py:574
  51.3 0.0 copy-done.1
  51.3 13.3 %shard_map.165 = (bf16[8,256,256]{2,1,0:T(8,128)(2,1)S(1)}, bf16[8,64,512]{2,1,0:T(8,128)(2,1)S(1)}, bf16[8,64,512]{2,1,0:T(8,128)(2,1)S(1)}, f32[64,512]{1,0:T(8,128)S(1)}, f32[16,64]{1,0:T(8,128)S(1)}) custom-call(s32[1,128]{1,0:T(1,128)S(1)} %get-tuple-element.33.slot_ref, s32[1]{0:T(128)} %bitcast.core_ref, ...), custom_call_target="tpu_custom_call" | custom-call | tf_op jit(solution)/shard_map/pallas_call | solution.py:86
  64.7 19.5 %all_to_all.26.parts_ref = bf16[8,256,256]{2,1,0:T(8,128)(2,1)S(1)} all-to-all(bf16[8,256,256]{2,1,0:T(8,128)(2,1)S(1)} %get-tuple-element.40), channel_id=1, replica_groups=mesh['dp'=16,'graph'=8] {'graph'}, dimensions={0} | all-to-all | bytes 2097152 | tf_op jit(solution)/shard_map/all_to_all | solution.py:578
  84.1 2.1 %shard_map.166 = (bf16[1024,512]{1,0:T(8,128)(2,1)S(1)}, bf16[8,112,512]{2,1,0:T(8,128)(2,1)S(1)}, bf16[8,112,512]{2,1,0:T(8,128)(2,1)S(1)}) custom-call(s32[1]{0:T(128)} %bitcast.core_ref, bf16[8,256,256]{2,1,0:T(8,128)(2,1)S(1)} %all_to_all.26.parts_ref, bf16[1024,512]{1,0:T(8,128)(2,1)S(1)} %copy-done, ...), custom_call_target="tpu_custom_call" | custom-call | tf_op jit(solution)/shard_map/pallas_call | solution.py:86
  86.3 0.1 collective-permute-start.1
  86.4 1.7 %shard_map.167 = bf16[1024,512]{1,0:T(8,128)(2,1)} custom-call(bf16[1024,512]{1,0:T(8,128)(2,1)S(1)} %get-tuple-element.47.dz_ref, bf16[512,640]{1,0:T(8,128)(2,1)S(1)} %get-tuple-element.41.weights_ref), custom_call_target="tpu_custom_call" | custom-call | tf_op jit(solution)/shard_map/pallas_call | solution.py:86
  88.1 0.8 collective-permute-done.1.other_ref
  88.8 0.2 shard_map.168
  89.0 17.4 %all_to_all.27.parts_ref = bf16[8,112,512]{2,1,0:T(8,128)(2,1)S(1)} all-to-all(bf16[8,112,512]{2,1,0:T(8,128)(2,1)S(1)} %shard_map.168), channel_id=1, replica_groups={{0,16,32,48,64,80,96,112},{8,24,40,56,72,88,104,120},{1,17,33,49,65,81,..., dimensions={0} | all-to-all | bytes 1835008 | tf_op jit(solution)/shard_map/all_to_all | solution.py:604
  106.4 0.1 shard_map.169.own_ref
  106.6 0.9 collective-permute-start.2
  107.5 5.4 %collective-permute-done.2.other_ref = bf16[112,512]{1,0:T(8,128)(2,1)S(1)} collective-permute-done((bf16[112,512]{1,0:T(8,128)(2,1)S(1)}, bf16[112,512]{1,0:T(8,128)(2,1)S(1)}, u32[]{:S(2)}, u32[]{:S(2)}) %collective-permute-start.2) | collective-permute-done | bytes 114720 | tf_op jit(solution)/shard_map/ppermute | solution.py:608
  113.0 10.1 %all_to_all.28.parts_ref = bf16[4,112,512]{2,1,0:T(8,128)(2,1)S(1)} all-to-all(bf16[4,112,512]{2,1,0:T(8,128)(2,1)S(1)} %shard_map.170), channel_id=1, replica_groups={{0,2,4,6},{1,3,5,7},{8,10,12,14},{9,11,13,15},{16,18,20,22},{17,19,21,2..., dimensions={0} | all-to-all | bytes 917504 | tf_op jit(solution)/shard_map/all_to_all | solution.py:613
  123.1 0.7 shard_map.171
  (1 shorter events, 0.0 us)
Async XLA Ops:
  2.5 6.5 %copy-start.2 = (bf16[16,8192]{1,0:T(8,128)(2,1)S(1)}, bf16[16,8192]{1,0:T(8,128)(2,1)}, u32[]{:S(2)}) copy-start(bf16[16,8192]{1,0:T(8,128)(2,1)} %basis_ref.1) | copy-start | bytes 786436
  2.5 6.5 %copy-start.3 = (s32[8192]{0:T(1024)S(1)}, s32[8192]{0:T(1024)}, u32[]{:S(2)}) copy-start(s32[8192]{0:T(1024)} %param.14) | copy-start | bytes 98308
  2.5 6.5 %copy-start.4 = (s32[8192]{0:T(1024)S(1)}, s32[8192]{0:T(1024)}, u32[]{:S(2)}) copy-start(s32[8192]{0:T(1024)} %param.15) | copy-start | bytes 98308
  2.6 23.3 %copy-start = (bf16[1024,512]{1,0:T(8,128)(2,1)S(1)}, bf16[1024,512]{1,0:T(8,128)(2,1)}, u32[]{:S(2)}) copy-start(bf16[1024,512]{1,0:T(8,128)(2,1)} %feats_ref.3) | copy-start | bytes 3145732
  2.6 20.8 %all-to-all-start = ((bf16[8,112,512]{2,1,0:T(8,128)(2,1)}), bf16[8,112,512]{2,1,0:T(8,128)(2,1)S(1)}, u32[]{:S(2)}, u32[]{:S(2)}) async-start(bf16[8,112,512]{2,1,0:T(8,128)(2,1)} %shard_map.162), calls=%async_computation | async-start | bytes 1835008 | tf_op jit(solution)/shard_map/all_to_all | solution.py:557
  23.3 2.5 %collective-permute-start = (bf16[8,112,512]{2,1,0:T(8,128)(2,1)S(1)}, bf16[8,112,512]{2,1,0:T(8,128)(2,1)S(1)}, u32[]{:S(2)}, u32[]{:S(2)}) collective-permute-start(bf16[8,112,512]{2,1,0:T(8,128)(2,1)S(1)} %all-to-all-done.own_ref), channel_id=1, source_target_pairs={{0,8},{8,0},{16,24},{24,16},{32,40},{40,32},{48,56},{56,48},{64,72... | collective-permute-start | bytes 2752520 | tf_op jit(solution)/shard_map/ppermute | solution.py:540
  27.3 24.1 %copy-start.1 = (bf16[1024,512]{1,0:T(8,128)(2,1)S(1)}, bf16[1024,512]{1,0:T(8,128)(2,1)}, u32[]{:S(2)}) copy-start(bf16[1024,512]{1,0:T(8,128)(2,1)} %cot_ref.1) | copy-start | bytes 3145732
  86.3 2.6 %collective-permute-start.1 = (bf16[8,112,512]{2,1,0:T(8,128)(2,1)S(1)}, bf16[8,112,512]{2,1,0:T(8,128)(2,1)S(1)}, u32[]{:S(2)}, u32[]{:S(2)}) collective-permute-start(bf16[8,112,512]{2,1,0:T(8,128)(2,1)S(1)} %get-tuple-element.46), channel_id=1, source_target_pairs={{0,8},{8,0},{16,24},{24,16},{32,40},{40,32},{48,56},{56,48},{64,72... | collective-permute-start | bytes 2752520 | tf_op jit(solution)/shard_map/ppermute | solution.py:540
  106.6 6.4 %collective-permute-start.2 = (bf16[112,512]{1,0:T(8,128)(2,1)S(1)}, bf16[112,512]{1,0:T(8,128)(2,1)S(1)}, u32[]{:S(2)}, u32[]{:S(2)}) collective-permute-start(bf16[112,512]{1,0:T(8,128)(2,1)S(1)} %shard_map.169.own_ref), channel_id=1, source_target_pairs={{0,1},{1,0},{2,3},{3,2},{4,5},{5,4},{6,7},{7,6},{8,9},{9,8},{10,11... | collective-permute-start | bytes 344072 | tf_op jit(solution)/shard_map/ppermute | solution.py:608
